TPU v7x, 128 devices: a whole 4x4x4 slice. The times are simulated.
128 devices in a mesh: hour: 2 (over core), bus: 16 (over x, y), line: 4 (over z).
Axes of the slice: x: 4, y: 4, z: 4, core: 2. Of those that a mesh axis runs over, the one named last changes fastest.
Arguments:
- ptdf: bfloat16 [19968, 16384], P('line', 'bus'), may hold values from -0.0625 to 0.0625
- units_out: float32 [192, 8, 4096], P('hour', None, 'bus'), may hold values from 0 to 1.5
- load: float32 [192, 8, 16384], P('hour', None, 'bus'), may hold values from -6 to 6
- unit_node: int32 [4096], P('bus'), may hold values from 0 to 16383, as said below
- commit_index: int32 [192, 4096], P('hour', 'bus'), may hold values from 0 to 3
- relax_levels: float32 [4], replicated, may hold values from 0.25 to 1
- line_active: int32 [192, 19968], P('hour', 'line'), may hold values 0 or 1
- line_limit: float32 [19968], P('line'), may hold values from 0.3 to 1.5
- line_weight: float32 [19968], P('line'), may hold values from 0.3 to 3
- ramp_active: int32 [192, 4096], P(None, 'bus'), may hold values 0 or 1
- ramp_limit: float32 [4096], P('bus'), may hold values from 0.05 to 0.4
- ramp_weight: float32 [4096], P('bus'), may hold values from 0.5 to 5
Outputs:
- units_grad: float32 [192, 8, 4096], P('hour', None, 'bus')
Inputs may be any that keep to these rules, and one draw needn't show every extreme that they name: `unit_node`: unit g sits at a node n with n // 1024 = g // 256.
All inputs are finite; a program needn't handle non-finite values. No bound on the sum of `line_active` or of `ramp_active` on one device may be relied on, other than what follows from the above.
Results may differ from a plain program's by a relative error of at most 0.0026.
Values may be sent and summed in bfloat16 or wider, within the bound.
A program may use at most 128 MiB of HBM per device.

v0:
```python
import jax
import jax.numpy as jnp
from jax import lax
from jax.sharding import PartitionSpec as P


def padded_2(block, sides, width):
    for axis, dim in sides:
        count = lax.axis_size(axis)
        forward = [(i, i + 1) for i in range(count - 1)]
        backward = [(target, source) for source, target in forward]
        low = lax.ppermute(
            lax.slice_in_dim(block, block.shape[dim] - width, None, axis=dim), axis, forward
        )
        high = lax.ppermute(lax.slice_in_dim(block, 0, width, axis=dim), axis, backward)
        block = jnp.concatenate([low, block, high], axis=dim)
    return block


def hinge_grad(values, limits):
    return jax.nn.relu(values - limits) - jax.nn.relu(-values - limits)


def body(
    ptdf,
    units_out,
    load,
    unit_node,
    commit_index,
    relax_levels,
    line_active,
    line_limit,
    line_weight,
    ramp_active,
    ramp_limit,
    ramp_weight,
):
    hours_dev, scenarios, units_dev = units_out.shape
    lines_dev, nodes_dev = ptdf.shape
    columns = hours_dev * scenarios
    bus_pos = lax.axis_index("bus")
    hour_pos = lax.axis_index("hour")
    level_ids = jnp.arange(relax_levels.shape[0], dtype=jnp.int32)
    unit_level = jnp.sum(
        jnp.where(commit_index[:, :, None] == level_ids, relax_levels, jnp.float32(0.0)), axis=-1
    )
    generation = unit_level[:, None, :] * units_out
    local_node = unit_node - bus_pos * nodes_dev
    placed = (
        jnp.zeros((columns, nodes_dev), jnp.float32)
        .at[:, local_node]
        .add(generation.reshape(columns, units_dev))
    )
    injection = (placed - load.reshape(columns, nodes_dev)).astype(jnp.bfloat16)
    active_full = jnp.repeat(line_active.T, scenarios, axis=1).astype(jnp.float32)
    share_rows = lines_dev // lax.axis_size("bus")
    ptdf_rows = ptdf
    flow_share = lax.psum_scatter(
        lax.dot_general(
            ptdf_rows, injection, (((1,), (1,)), ((), ())), preferred_element_type=jnp.float32
        ),
        "bus",
        scatter_dimension=0,
        tiled=True,
    )
    first_row = bus_pos * share_rows
    row_count = flow_share.shape[0]
    active = lax.dynamic_slice_in_dim(active_full, first_row, row_count, 0)
    limits = lax.dynamic_slice_in_dim(line_limit, first_row, row_count, 0)
    scales = lax.dynamic_slice_in_dim(line_weight, first_row, row_count, 0)
    weights = 2.0 * scales[:, None] * active
    grad_share = (weights * hinge_grad(flow_share, limits[:, None])).astype(jnp.bfloat16)
    ptdf_rows = ptdf
    node_part = lax.dot_general(
        lax.all_gather(grad_share, "bus", axis=0, tiled=True),
        ptdf_rows,
        (((0,), (0,)), ((), ())),
        preferred_element_type=jnp.float32,
    )
    node_grad = lax.psum(node_part, "line")
    unit_grad = jnp.take(node_grad, local_node, axis=1).reshape(hours_dev, scenarios, units_dev)
    hours_all = hours_dev * lax.axis_size("hour")
    padded = padded_2(generation, (("hour", 0),), 1)
    ramp_step = padded[1:] - padded[:-1]
    hour_ids = hour_pos * hours_dev + jnp.arange(hours_dev + 1, dtype=jnp.int32)
    inside = ((hour_ids >= 1) & (hour_ids <= hours_all - 1)).astype(jnp.float32)
    extended = jnp.concatenate([ramp_active, jnp.zeros((1, units_dev), jnp.int32)], axis=0)
    ramp_rows = lax.dynamic_slice_in_dim(extended, hour_pos * hours_dev, hours_dev + 1, 0).astype(
        jnp.float32
    )
    ramp_mask = (ramp_rows * inside[:, None])[:, None, :]
    ramp_dual = 2.0 * ramp_weight * ramp_mask * hinge_grad(ramp_step, ramp_limit)
    return unit_level[:, None, :] * (unit_grad + ramp_dual[:-1] - ramp_dual[1:])


def solution(mesh):
    return jax.shard_map(
        body,
        mesh=mesh,
        in_specs=(
            P("line", "bus"),
            P("hour", None, "bus"),
            P("hour", None, "bus"),
            P("bus"),
            P("hour", "bus"),
            P(),
            P("hour", "line"),
            P("line"),
            P("line"),
            P(None, "bus"),
            P("bus"),
            P("bus"),
        ),
        out_specs=P("hour", None, "bus"),
        check_vma=False,
    )
```

profile of v0, /device:TPU:0, one launch (start us, length us, event | category | flops | bytes accessed | tf_op | source)
XLA Modules:
  0.0 420.1 jit_solution(1041295639683977550)
XLA Ops:
  6.5 1.2 select_reduce_fusion
  7.7 2.1 fusion.12
  9.8 2.3 copy.26
  12.1 2.3 copy.27
  14.5 4.8 %scatter_custom_fusion = f32[768,1024]{0,1:T(8,128)} fusion(s32[256]{0:T(256)S(1)} %get-tuple-element.6, f32[]{:T(128)} %constant.16.clone.1, f32[768,256]{0,1:T(8,128)} %copy.26), kind=kCustom, calls=%fused_computation.6 | custom fusion | flops 196608 | bytes 3932164 | tf_op jit(solution)/shard_map/scatter-add | solution.py:52
  19.3 16.1 %convolution_bitcast_fusion = f32[4992,768]{0,1:T(8,128)} fusion(bf16[4992,1024]{1,0:T(8,128)(2,1)} %param.12, f32[768,1024]{0,1:T(8,128)} %scatter_custom_fusion, f32[768,1024]{0,1:T(8,128)S(1)} %copy-done.1), kind=kOutput, calls=%fused_computation.2 | convolution fusion | flops 7853309952 | bytes 31850496 | tf_op jit(solution)/shard_map/dot_general | solution.py:59
  35.5 0.9 dynamic_slice.14
  37.6 0.8 dynamic-slice_multiply_fusion
  38.5 6.3 %broadcast_bitcast_fusion = f32[4992,768]{0,1:T(8,128)} fusion(f32[4992,96]{0,1:T(8,128)S(1)} %convert_bitcast_fusion), kind=kLoop, calls=%fused_computation.3 | loop fusion | bytes 17252352 | tf_op jit(solution)/shard_map/convert_element_type | solution.py:55
  44.8 199.0 %all-reduce.7.cloned.1.call-done = f32[4992,768]{0,1:T(8,128)} async-done(((f32[4992,768]{0,1:T(8,128)}), f32[4992,768]{0,1:T(8,128)}) %all-reduce.7.cloned.1.call-update) | async-done | bytes 15335440
  243.8 2.6 multiply_convert_fusion
  246.4 1.0 copy.28
  247.7 67.3 %all-gather.2.cloned.1.call-done = bf16[4992,768]{1,0:T(8,128)(2,1)} async-done(((bf16[312,768]{1,0:T(8,128)(2,1)}), bf16[4992,768]{1,0:T(8,128)(2,1)}) %all-gather.2.cloned.1.call-update) | async-done | bytes 7667728 | tf_op jit(solution)/shard_map/all_gather | solution.py:75
  315.0 14.4 %fusion.8 = f32[768,1024]{1,0:T(8,128)} fusion(bf16[4992,768]{1,0:T(8,128)(2,1)} %all-gather.2.cloned.1.call-done, bf16[4992,1024]{1,0:T(8,128)(2,1)} %param.12), kind=kOutput, calls=%fused_computation.30 | convolution fusion | flops 7851737088 | bytes 21037056 | tf_op jit(solution)/shard_map/dot_general | solution.py:74
  329.4 1.1 copy-done.2
  330.6 1.3 collective-permute-start
  331.9 3.0 collective-permute-start.1
  335.1 0.6 collective-permute-done.1
  335.8 1.1 subtract_multiply_fusion
  336.9 68.5 %all-reduce.5.cloned.1.call-done = f32[768,1024]{1,0:T(8,128)} async-done(((f32[768,1024]{1,0:T(8,128)}), f32[768,1024]{1,0:T(8,128)}) %all-reduce.5.cloned.1.call-update) | async-done | bytes 3145744 | tf_op jit(solution)/shard_map/psum | solution.py:80
  405.3 2.4 copy.29
  407.7 2.0 gather_fusion
  409.7 1.4 copy.30
  411.1 2.4 fusion.2
  (33 shorter events, 1.3 us)
Async XLA Ops:
  6.5 5.6 %copy-start = (f32[96,8,1024]{2,1,0:T(8,128)S(1)}, f32[96,8,1024]{2,1,0:T(8,128)}, u32[]{:S(2)}) copy-start(f32[96,8,1024]{2,1,0:T(8,128)} %param.14) | copy-start | bytes 9437188
  6.5 237.3 %all-reduce.7.cloned.1.call-start = ((), (), s32[]{:S(2)}) async-start(), calls=%async_computation.2 | async-start | bytes 30670848
  12.1 2.3 copy-start.6
  14.4 4.8 %copy-start.1 = (f32[768,1024]{0,1:T(8,128)S(1)}, f32[768,1024]{0,1:T(8,128)}, u32[]{:S(2)}) copy-start(f32[768,1024]{0,1:T(8,128)} %copy.27) | copy-start | bytes 9437188
  35.4 1.0 copy-start.8
  35.4 3.0 copy-start.3
  35.4 279.5 %all-gather.2.cloned.1.call-start = ((), (), s32[]{:S(2)}) async-start(), calls=%async_computation | async-start | bytes 8146944 | tf_op jit(solution)/shard_map/all_gather | solution.py:75
  247.5 157.9 %all-reduce.5.cloned.1.call-start = ((), (), s32[]{:S(2)}) async-start(), calls=%async_computation.1 | async-start | bytes 6291456 | tf_op jit(solution)/shard_map/psum | solution.py:80
  329.4 1.1 copy-start.2
  329.4 5.6 %copy-start.7 = (f32[256]{0:T(256)S(1)}, f32[256]{0:T(256)}, u32[]{:S(2)}) copy-start(f32[256]{0:T(256)} %param.23) | copy-start | bytes 3076
  329.4 5.6 %copy-start.4 = (s32[192,256]{1,0:T(8,128)S(1)}, s32[192,256]{1,0:T(8,128)}, u32[]{:S(2)}) copy-start(s32[192,256]{1,0:T(8,128)} %param.21) | copy-start | bytes 589828
  329.4 6.4 %copy-start.5 = (f32[256]{0:T(256)S(1)}, f32[256]{0:T(256)}, u32[]{:S(2)}) copy-start(f32[256]{0:T(256)} %param.22) | copy-start | bytes 3076
  330.6 4.5 %collective-permute-start = (f32[1,8,256]{2,1,0:T(8,128)S(1)}, f32[1,8,256]{2,1,0:T(8,128)S(1)}, u32[]{:S(2)}, u32[]{:S(2)}) collective-permute-start(f32[1,8,256]{2,1,0:T(8,128)S(1)} %get-tuple-element.7), channel_id=1, source_target_pairs={{64,0},{65,1},{66,2},{67,3},{68,4},{69,5},{70,6},{71,7},{72,8},{73... | collective-permute-start | bytes 24584 | tf_op jit(solution)/shard_map/ppermute | solution.py:15
  331.9 3.8 collective-permute-start.1
Sparse Core Ops, SparseCore 0:
  35.5 208.2 all-reduce.6
  247.6 67.3 all-gather.1
  329.5 75.7 all-reduce.4
where the time goes:
time: 421 us; the launch traced here: 420 us
  waiting for transfers between devices  335 us (80%)
  matrix products  30.5 us (7%)
  local copies, waits for them, and re-layouts  20.3 us (5%)
  other arithmetic  15.3 us (4%)
  between operations  13.9 us (3%)
  starting transfers between devices  4.58 us (1%)
    unnamed x4, waiting for transfers between devices  199 us
    psum x1, waiting for transfers between devices, body(): node_grad = lax.psum(node_part, 'line')  68.5 us
    all_gather x1, waiting for transfers between devices, body(): lax.all_gather(grad_share, 'bus', axis=0, tiled=True)  67.3 us
    dot_general x1, matrix products, body(): lax.dot_general(ptdf_rows, injection, (((1,), (1,)), ((), ())), preferred...  16.1 us
    dot_general x1, matrix products, body(): lax.dot_general(lax.all_gather(grad_share, 'bus', axis=0, tiled=True), pt...  14.4 us
  transfers between devices with their start and end apart: 5, of which 4 were waited for; matrix products, arithmetic and copies ran while one was open for 2% of the time, Pallas kernels for 0%

commit v1 on v0

v1 whole, which is shorter than its diff:
```python
import functools

import jax
import jax.numpy as jnp
from jax import lax
from jax.experimental import pallas as pl
from jax.experimental.pallas import tpu as pltpu
from jax.sharding import PartitionSpec as P

MESH = pl.DeviceIdType.MESH
F32 = jnp.float32
BF16 = jnp.bfloat16

CHUNKS = 6
QUARTER = 1280
HALF = 640
S1A, S1B, S2A, S2B, AGY, SUMZ, SUMX, AGZ = range(8)
KINDS = 8


def hinge_grad(values, limits):
    return jnp.maximum(values - limits, 0.0) - jnp.maximum(-values - limits, 0.0)


def kernel(
    ptdf_hbm, inj, node, act, lim, out,
    p, part_a, part_b, land_a, land_b, sum_a, sum_b, land2_a, land2_b, fg, u,
    land_z, sum_z, land_x, ob, onehot, g_send, g, p_sem, ssem, rsem, gs_sem, gr_sem, cs_sem, cr_sem,
):
    chunk = part_a.shape[2]
    sub = chunk // 4
    lines = ptdf_hbm.shape[0] // 4
    units = node.shape[1]
    hour = lax.axis_index("hour")
    bus = lax.axis_index("bus")
    z = lax.axis_index("line")
    x = bus // 4
    y = bus % 4

    def at(pos, j):
        return lax.rem(pos + (1, 3, 2)[j], 4)

    def dev_x(j):
        return (hour, at(x, j) * 4 + y, z)

    def dev_y(j):
        return (hour, x * 4 + at(y, j), z)

    def dev_z(j):
        return (hour, bus, at(z, j))

    sibling = (1 - hour, bus, z)

    def rows(pos):
        return pl.ds(pl.multiple_of(pos * sub, sub), sub)

    def lanes(pos):
        return pl.ds(pl.multiple_of(pos * units, units), units)

    def copy(kind, j, c):
        if kind == S1A:
            src, dst, dev = part_a.at[c, at(x, j)], land_a.at[c, j], dev_x(j)
        elif kind == S1B:
            src, dst, dev = part_b.at[c, :, rows(at(y, j))], land_b.at[c, j], dev_y(j)
        elif kind == S2A:
            src, dst, dev = sum_a.at[c, rows(at(y, j))], land2_a.at[c, j], dev_y(j)
        elif kind == S2B:
            src, dst, dev = sum_b.at[c, at(x, j)], land2_b.at[c, j], dev_x(j)
        elif kind == AGY:
            src, dst, dev = fg.at[c, rows(y)], fg.at[c, rows(y)], dev_y(j)
        elif kind == SUMZ:
            src, dst, dev = u.at[c, rows(at(z, j))], land_z.at[c, j], dev_z(j)
        elif kind == SUMX:
            src, dst, dev = sum_z.at[c, :, lanes(at(x, j))], land_x.at[c, j], dev_x(j)
        else:
            src, dst, dev = ob.at[c, rows(z)], ob.at[c, rows(z)], dev_z(j)
        return pltpu.make_async_remote_copy(
            src_ref=src, dst_ref=dst, send_sem=ssem.at[kind, j, c], recv_sem=rsem.at[kind, j, c],
            device_id=dev, device_id_type=MESH,
        )

    def send(kind, c):
        for j in (2, 0, 1):
            copy(kind, j, c).start()

    def receive(kind, c):
        for j in range(3):
            copy(kind, j, c).wait_recv()

    def load(q):
        return pltpu.make_async_copy(
            ptdf_hbm.at[pl.ds(pl.multiple_of(q * lines, 16), lines)],
            p.at[q, pl.ds(0, lines)], p_sem.at[q],
        )

    def g_rows(h):
        return pl.ds(pl.multiple_of(h * HALF, HALF), HALF)

    def g_copy(j):
        return pltpu.make_async_remote_copy(
            src_ref=g_send.at[j], dst_ref=g.at[x, g_rows(hour)], send_sem=gs_sem.at[j],
            recv_sem=gr_sem.at[j], device_id=dev_x(j), device_id_type=MESH,
        )

    def g_share(j):
        source = at(x, (1, 0, 2)[j])
        return pltpu.make_async_remote_copy(
            src_ref=g.at[source, g_rows(hour)], dst_ref=g.at[source, g_rows(hour)],
            send_sem=cs_sem.at[j], recv_sem=cr_sem.at[j], device_id=sibling, device_id_type=MESH,
        )

    def flows(c):
        columns = inj[pl.ds(pl.multiple_of(c * chunk, chunk), chunk), :]
        for k in range(4):
            q = lax.rem(x + 1 + k, 4)
            for half, part in ((0, part_a), (1, part_b)):
                part[c, q] = lax.dot_general(
                    columns, p[q, half * HALF : (half + 1) * HALF, :], (((1,), (1,)), ((), ())),
                    preferred_element_type=F32,
                ).astype(BF16)
        send(S1A, c)
        send(S1B, c)

    def step1(c):
        receive(S1A, c)
        total = part_a[c, x].astype(F32)
        for j in range(3):
            total = total + land_a[c, j].astype(F32)
        sum_a[c] = total.astype(BF16)
        send(S2A, c)
        receive(S1B, c)
        total = part_b[c, :, rows(y), :].astype(F32)
        for j in range(3):
            total = total + land_b[c, j].astype(F32)
        sum_b[c] = total.astype(BF16)
        send(S2B, c)

    def step2(c):
        receive(S2A, c)
        total = part_a[c, x, rows(y), :].astype(F32)
        for j in range(3):
            total = total + land_a[c, j, rows(y), :].astype(F32)
        for j in range(3):
            total = total + land2_a[c, j].astype(F32)
        fg[c, rows(y), 0:HALF] = (act[c, :, 0:HALF] * hinge_grad(total, lim[:, 0:HALF])).astype(BF16)
        receive(S2B, c)
        total = part_b[c, x, rows(y), :].astype(F32)
        for j in range(3):
            total = total + land_b[c, j, x].astype(F32)
        for j in range(3):
            total = total + land2_b[c, j].astype(F32)
        fg[c, rows(y), HALF:QUARTER] = (
            act[c, :, HALF:QUARTER] * hinge_grad(total, lim[:, HALF:QUARTER])
        ).astype(BF16)
        send(AGY, c)

    def step3(c):
        receive(AGY, c)
        for k in range(4):
            u[c, :, k * units : (k + 1) * units] = jnp.dot(
                fg[c], g[k], preferred_element_type=F32
            )
        send(SUMZ, c)

    def step4(c):
        receive(SUMZ, c)
        total = u[c, rows(z), :]
        for j in range(3):
            total = total + land_z[c, j]
        sum_z[c] = total
        send(SUMX, c)

    def step5(c):
        receive(SUMX, c)
        total = sum_z[c, :, lanes(x)]
        for j in range(3):
            total = total + land_x[c, j]
        ob[c, rows(z), :] = total
        send(AGZ, c)

    def step6(c):
        receive(AGZ, c)
        out[pl.ds(pl.multiple_of(c * chunk, chunk), chunk), :] = ob[c]
        for kind in range(KINDS):
            for j in range(3):
                copy(kind, j, c).wait_send()

    for q in range(4):
        load(q).start()
    barrier = pltpu.get_barrier_semaphore()
    for j in range(3):
        for dev in (dev_x(j), dev_y(j), dev_z(j)):
            pl.semaphore_signal(barrier, inc=1, device_id=dev, device_id_type=MESH)
    pl.semaphore_signal(barrier, inc=1, device_id=sibling, device_id_type=MESH)
    p[:, lines:QUARTER, :] = jnp.zeros((4, QUARTER - lines, p.shape[2]), BF16)
    onehot[...] = (
        lax.broadcasted_iota(jnp.int32, onehot.shape, 0) == node[...]
    ).astype(F32).astype(BF16)
    pl.semaphore_wait(barrier, 10)
    for q in range(4):
        load(q).wait()
    flows(0)
    for j in range(3):
        g_send[j] = jnp.dot(
            p[at(x, j), g_rows(hour), :], onehot[...], preferred_element_type=F32
        ).astype(BF16)
        g_copy(j).start()
    g[x] = jnp.dot(p[x], onehot[...], preferred_element_type=F32).astype(BF16)

    def body(i, carry):
        @pl.when(i >= 6)
        def _():
            step6(i - 6)

        @pl.when((i >= 5) & (i < CHUNKS + 5))
        def _():
            step5(i - 5)

        @pl.when((i >= 4) & (i < CHUNKS + 4))
        def _():
            step4(i - 4)

        @pl.when(i == 3)
        def _():
            for j in range(3):
                g_share(j).wait_recv()

        @pl.when((i >= 3) & (i < CHUNKS + 3))
        def _():
            step3(i - 3)

        @pl.when((i >= 2) & (i < CHUNKS + 2))
        def _():
            step2(i - 2)

        @pl.when(i == 2)
        def _():
            for j in range(3):
                g_copy(j).wait_recv()
                g_share(j).start()

        @pl.when(i < CHUNKS + 1)
        def _():
            step1(i - 1)

        @pl.when(i < CHUNKS)
        def _():
            flows(i)

        return carry

    lax.fori_loop(1, CHUNKS + 6, body, 0)
    for j in range(3):
        g_copy(j).wait_send()
        g_share(j).wait_send()


def node_gradient(ptdf, inj, node, act, lim):
    columns, nodes = inj.shape
    units = node.shape[1]
    chunk = columns // CHUNKS
    sub = chunk // 4
    vmem = pl.BlockSpec(memory_space=pltpu.VMEM)
    dma = pltpu.SemaphoreType.DMA
    return pl.pallas_call(
        kernel,
        out_shape=jax.ShapeDtypeStruct((columns, units), F32),
        in_specs=[pl.BlockSpec(memory_space=pl.ANY), vmem, vmem, vmem, vmem],
        out_specs=vmem,
        scratch_shapes=[
            pltpu.VMEM((4, QUARTER, nodes), BF16),
            pltpu.VMEM((CHUNKS, 4, chunk, HALF), BF16),
            pltpu.VMEM((CHUNKS, 4, chunk, HALF), BF16),
            pltpu.VMEM((CHUNKS, 3, chunk, HALF), BF16),
            pltpu.VMEM((CHUNKS, 3, 4, sub, HALF), BF16),
            pltpu.VMEM((CHUNKS, chunk, HALF), BF16),
            pltpu.VMEM((CHUNKS, 4, sub, HALF), BF16),
            pltpu.VMEM((CHUNKS, 3, sub, HALF), BF16),
            pltpu.VMEM((CHUNKS, 3, sub, HALF), BF16),
            pltpu.VMEM((CHUNKS, chunk, QUARTER), BF16),
            pltpu.VMEM((CHUNKS, chunk, 4 * units), F32),
            pltpu.VMEM((CHUNKS, 3, sub, 4 * units), F32),
            pltpu.VMEM((CHUNKS, sub, 4 * units), F32),
            pltpu.VMEM((CHUNKS, 3, sub, units), F32),
            pltpu.VMEM((CHUNKS, chunk, units), F32),
            pltpu.VMEM((nodes, units), BF16),
            pltpu.VMEM((3, HALF, units), BF16),
            pltpu.VMEM((4, QUARTER, units), BF16),
            dma((4,)),
            dma((KINDS, 3, CHUNKS)),
            dma((KINDS, 3, CHUNKS)),
            dma((3,)),
            dma((3,)),
            dma((3,)),
            dma((3,)),
        ],
        compiler_params=pltpu.CompilerParams(
            collective_id=0, has_side_effects=True, vmem_limit_bytes=60 << 20
        ),
    )(ptdf, inj, node, act, lim)


def body(
    ptdf, units_out, load, unit_node, commit_index, relax_levels,
    line_active, line_limit, line_weight, ramp_active, ramp_limit, ramp_weight,
):
    hours_dev, scenarios, units_dev = units_out.shape
    lines_dev, nodes_dev = ptdf.shape
    columns = hours_dev * scenarios
    bus_pos = lax.axis_index("bus")
    hour_pos = lax.axis_index("hour")
    x, y = bus_pos // 4, bus_pos % 4
    level_ids = jnp.arange(relax_levels.shape[0], dtype=jnp.int32)
    unit_level = jnp.sum(
        jnp.where(commit_index[:, :, None] == level_ids, relax_levels, jnp.float32(0.0)), axis=-1
    )
    generation = unit_level[:, None, :] * units_out
    local_node = unit_node - bus_pos * nodes_dev
    onehot = (local_node[:, None] == jnp.arange(nodes_dev, dtype=jnp.int32)).astype(F32)
    placed = jnp.dot(
        generation.reshape(columns, units_dev), onehot, precision=lax.Precision.HIGHEST
    )
    injection = (placed - load.reshape(columns, nodes_dev)).astype(BF16)

    lines = lines_dev // 4
    sub_hours = hours_dev // CHUNKS // 4

    def own_lines(array):
        block = lax.dynamic_slice_in_dim(array, x * lines, lines, -1)
        pad = [(0, 0)] * (block.ndim - 1) + [(0, QUARTER - lines)]
        return jnp.pad(block, pad)

    active = lax.dynamic_slice_in_dim(
        line_active.reshape(CHUNKS, 4, sub_hours, lines_dev), y, 1, 1
    )[:, 0]
    active = own_lines(active).astype(F32)
    weights = own_lines(2.0 * line_weight) * active
    act = jnp.repeat(weights, scenarios, axis=1)
    lim = own_lines(line_limit)[None, :]
    unit_grad = node_gradient(ptdf, injection, local_node[None, :], act, lim).reshape(
        hours_dev, scenarios, units_dev
    )

    hours_all = hours_dev * lax.axis_size("hour")
    low = lax.ppermute(generation[-1:], "hour", [(0, 1)])
    high = lax.ppermute(generation[:1], "hour", [(1, 0)])
    padded = jnp.concatenate([low, generation, high], axis=0)
    ramp_step = padded[1:] - padded[:-1]
    hour_ids = hour_pos * hours_dev + jnp.arange(hours_dev + 1, dtype=jnp.int32)
    inside = ((hour_ids >= 1) & (hour_ids <= hours_all - 1)).astype(F32)
    extended = jnp.concatenate([ramp_active, jnp.zeros((1, units_dev), jnp.int32)], axis=0)
    ramp_rows = lax.dynamic_slice_in_dim(
        extended, hour_pos * hours_dev, hours_dev + 1, 0
    ).astype(F32)
    ramp_mask = (ramp_rows * inside[:, None])[:, None, :]
    ramp_dual = 2.0 * ramp_weight * ramp_mask * hinge_grad(ramp_step, ramp_limit)
    return unit_level[:, None, :] * (unit_grad + ramp_dual[:-1] - ramp_dual[1:])


def solution(mesh):
    return jax.shard_map(
        body,
        mesh=mesh,
        in_specs=(
            P("line", "bus"),
            P("hour", None, "bus"),
            P("hour", None, "bus"),
            P("bus"),
            P("hour", "bus"),
            P(),
            P("hour", "line"),
            P("line"),
            P("line"),
            P(None, "bus"),
            P("bus"),
            P("bus"),
        ),
        out_specs=P("hour", None, "bus"),
        check_vma=False,
    )
```

time: 421 us -> 147 us (0.35)
  waiting for transfers between devices: 335 us -> 0.01 us
  Pallas kernels: 0 us -> 127 us
  matrix products: 30.5 us -> 4.7 us
  local copies, waits for them, and re-layouts: 20.3 us -> 4.48 us
  between operations: 13.9 us -> 0.21 us
  other arithmetic: 15.3 us -> 5.51 us
    unnamed x4 -> x0, waiting for transfers between devices: 199 us -> none
    pallas_call x0 -> x1, Pallas kernels: none -> 127 us  [node_gradient(): pl.pallas_call(kernel, out_shape=jax.ShapeDtypeStruct((columns, units), F...]
    psum x1 -> x0, waiting for transfers between devices: 68.5 us -> none  [body(): node_grad = lax.psum(node_part, 'line')]
    all_gather x1 -> x0, waiting for transfers between devices: 67.3 us -> none  [body(): lax.all_gather(grad_share, 'bus', axis=0, tiled=True)]
    dot_general x2 -> x1, matrix products: 30.5 us -> 4.7 us  [body(): jnp.dot(generation.reshape(columns, units_dev), onehot, precision=lax.Pre...]
    convert_element_type x2 -> x0, local copies, waits for them, and re-layouts: 7.3 us -> none  [the longest x1 6.29 us: body(): jnp.repeat(line_active.T, scenarios, axis=1).astype(jnp.float32)]
    scatter-add x1 -> x0, other arithmetic: 4.83 us -> none  [body(): placed = jnp.zeros((columns, nodes_dev), jnp.float32).at[:, local_node].a...]
  transfers between devices with their start and end apart: 5 -> 2, of which waited for: 4 -> 0; matrix products, arithmetic and copies ran while one was open for 2% -> 7% of each run, Pallas kernels for 0% -> 87%
where the time goes in v1:
time: 147 us; the launch traced here: 146 us
  Pallas kernels  127 us (86%)
  other arithmetic  5.51 us (4%)
  matrix products  4.7 us (3%)
  local copies, waits for them, and re-layouts  4.48 us (3%)
  starting transfers between devices  4.32 us (3%)
    pallas_call x1, Pallas kernels, node_gradient(): pl.pallas_call(kernel, out_shape=jax.ShapeDtypeStruct((columns, units), F...  127 us
    dot_general x1, matrix products, body(): jnp.dot(generation.reshape(columns, units_dev), onehot, precision=lax.Pre...  4.7 us
    ppermute x1, starting transfers between devices, body(): low = lax.ppermute(generation[-1:], 'hour', [(0, 1)])  3.03 us
  transfers between devices with their start and end apart: 2, of which 0 were waited for; matrix products, arithmetic and copies ran while one was open for 7% of the time, Pallas kernels for 87%

profile of v1, /device:TPU:0, one launch (start us, length us, event | category | flops | bytes accessed | tf_op | source)
XLA Modules:
  0.0 146.4 jit_solution(1313137792830258265)
XLA Ops:
  0.0 1.0 select_reduce_fusion
  1.0 1.2 broadcast_multiply_fusion
  2.3 0.0 copy-start.3
  2.3 0.0 copy-start.4
  2.3 1.3 collective-permute-start
  3.6 3.0 %collective-permute-start.1 = (f32[1,8,256]{2,1,0:T(8,128)S(1)}, f32[1,8,256]{2,1,0:T(8,128)S(1)}, u32[]{:S(2)}, u32[]{:S(2)}) collective-permute-start(f32[1,8,256]{2,1,0:T(8,128)S(1)} %get-tuple-element.6), channel_id=1, source_target_pairs={{0,64},{1,65},{2,66},{3,67},{4,68},{5,69},{6,70},{7,71},{8,72},{9,... | collective-permute-start | bytes 24584 | tf_op jit(solution)/shard_map/ppermute | solution.py:345
  6.7 1.9 %reshape.36 = s32[6,4,4,4992]{3,2,1,0:T(4,128)S(1)} reshape(s32[96,4992]{1,0:T(8,128)} %param.18) | data formatting | bytes 3833856 | tf_op jit(solution)/shard_map/reshape | solution.py:334
  8.6 0.8 dynamic-slice_multiply_fusion
  9.4 0.1 dynamic-slice_bitcast_fusion
  9.6 0.0 copy-start
  9.6 1.0 broadcast_bitcast_fusion.act
  10.6 0.0 copy-done.3
  10.6 0.0 copy-done.4
  10.6 0.0 copy-start.1
  10.6 4.7 %fusion.inj = bf16[768,1024]{1,0:T(8,128)(2,1)} fusion(f32[96,8,1024]{2,1,0:T(8,128)} %param.14, f32[96,8,256]{2,1,0:T(8,128)S(1)} %broadcast_multiply_fusion, s32[256]{0:T(256)S(1)} %broadcast_subtract_fusion), kind=kOutput, calls=%fused_computation.1 | convolution fusion | flops 2417754112 | bytes 5506048 | tf_op jit(solution)/shard_map/dot_general | solution.py:320
  15.3 0.1 fusion.6
  15.4 0.8 dynamic_slice.18
  16.2 0.6 broadcast_in_dim.18.lim
  16.8 127.2 %shard_map.118 = f32[768,256]{1,0:T(8,128)} custom-call(bf16[4992,1024]{1,0:T(8,128)(2,1)} %ptdf_hbm.1, bf16[768,1024]{1,0:T(8,128)(2,1)} %fusion.inj, s32[1,256]{1,0:T(1,128)} %bitcast.14, f32[6,32,1280]{2,1,0:T(8,128)} %broadcast_bitcast_fusion.act, f32[1,1280]{1,0:T(1,128)} %broadcast_in_dim.18.lim), custom_call_target="tpu_custom_call" | custom-call | tf_op jit(solution)/shard_map/pallas_call | solution.py:265
  144.0 0.0 collective-permute-done
  144.0 0.0 collective-permute-done.1
  144.0 0.0 copy-done.2
  144.1 0.2 subtract_multiply_fusion
  144.3 2.1 %fusion.1 = f32[96,8,256]{2,1,0:T(8,128)} fusion(f32[97,8,256]{2,1,0:T(8,128)S(1)} %subtract_multiply_fusion, f32[768,256]{1,0:T(8,128)} %shard_map.118, f32[96,256]{1,0:T(8,128)S(1)} %select_reduce_fusion), kind=kLoop, calls=%fused_computation.6 | loop fusion | flops 589824 | bytes 3244032 | tf_op jit(solution)/shard_map/mul | solution.py:357
  (10 shorter events, 0.1 us)
Async XLA Ops:
  2.3 8.3 %copy-start.3 = (f32[256]{0:T(256)S(1)}, f32[256]{0:T(256)}, u32[]{:S(2)}) copy-start(f32[256]{0:T(256)} %param.23) | copy-start | bytes 3076
  2.3 8.3 %copy-start.4 = (s32[256]{0:T(256)S(1)}, s32[256]{0:T(256)}, u32[]{:S(2)}) copy-start(s32[256]{0:T(256)} %param.15) | copy-start | bytes 3076
  2.3 141.7 %collective-permute-start = (f32[1,8,256]{2,1,0:T(8,128)S(1)}, f32[1,8,256]{2,1,0:T(8,128)S(1)}, u32[]{:S(2)}, u32[]{:S(2)}) collective-permute-start(f32[1,8,256]{2,1,0:T(8,128)S(1)} %get-tuple-element.5), channel_id=1, source_target_pairs={{64,0},{65,1},{66,2},{67,3},{68,4},{69,5},{70,6},{71,7},{72,8},{73... | collective-permute-start | bytes 24584 | tf_op jit(solution)/shard_map/ppermute | solution.py:346
  3.6 140.4 %collective-permute-start.1 = (f32[1,8,256]{2,1,0:T(8,128)S(1)}, f32[1,8,256]{2,1,0:T(8,128)S(1)}, u32[]{:S(2)}, u32[]{:S(2)}) collective-permute-start(f32[1,8,256]{2,1,0:T(8,128)S(1)} %get-tuple-element.6), channel_id=1, source_target_pairs={{0,64},{1,65},{2,66},{3,67},{4,68},{5,69},{6,70},{7,71},{8,72},{9,... | collective-permute-start | bytes 24584 | tf_op jit(solution)/shard_map/ppermute | solution.py:345
  9.6 5.8 %copy-start = (s32[192,256]{1,0:T(8,128)S(1)}, s32[192,256]{1,0:T(8,128)}, u32[]{:S(2)}) copy-start(s32[192,256]{1,0:T(8,128)} %param.21) | copy-start | bytes 589828
  10.6 6.2 %copy-start.1 = (s32[256]{0:T(256)}, s32[256]{0:T(256)S(1)}, u32[]{:S(2)}) copy-start(s32[256]{0:T(256)S(1)} %broadcast_subtract_fusion) | copy-start | bytes 3076
  16.8 127.2 %copy-start.2 = (f32[256]{0:T(256)S(1)}, f32[256]{0:T(256)}, u32[]{:S(2)}) copy-start(f32[256]{0:T(256)} %param.22) | copy-start | bytes 3076

commit v2 on v1

v2 whole, which is shorter than its diff:
```python
import jax
import jax.numpy as jnp
from jax import lax
from jax.experimental import pallas as pl
from jax.experimental.pallas import tpu as pltpu
from jax.sharding import PartitionSpec as P

MESH = pl.DeviceIdType.MESH
F32 = jnp.float32
BF16 = jnp.bfloat16

CHUNKS = 6
BLOCK = 128
HALF = 640
QUARTER = 2 * HALF
SCEN = 8
OA, DA, RA, OB, DB, RB, S2A, S2B, AGY, SUMZ, SUMX, AGZ = range(12)
KINDS = 12
WIDE = (S2A, S2B, AGY, SUMZ, SUMX, AGZ)


def hinge_grad(values, limits):
    return jnp.maximum(values - limits, 0.0) - jnp.maximum(-values - limits, 0.0)


def kernel(
    levels, ptdf_hbm, load_hbm, units_hbm, commit_hbm, active_hbm, ramp_hbm,
    node, limit, weight, ramp_limit, ramp_weight, out,
    p, load, units, commit, active, ramp, lev, gx, rw, lim, wgt, inj,
    part_a, part_b, own_a, relay_a, relay_b, land_a, land_b, sum_a, sum_b, land2_a, land2_b,
    fg, u, land_z, sum_z, land_x, ob, onehot, g_send, g,
    p_sem, in_sem, ssem, rsem, gs_sem, gr_sem, cs_sem, cr_sem, halo_sem,
):
    columns, nodes = load.shape
    hours = columns // SCEN
    lines = ptdf_hbm.shape[0]
    n_units = node.shape[1]
    chunk = columns // CHUNKS
    sub = chunk // 4
    hour = lax.axis_index("hour")
    bus = lax.axis_index("bus")
    z = lax.axis_index("line")
    x = bus // 4
    y = bus % 4
    sibling = (1 - hour, bus, z)

    def at(pos, j):
        return lax.rem(pos + (1, 3, 2)[j], 4)

    def dev_x(j):
        return (hour, at(x, j) * 4 + y, z)

    def dev_y(j):
        return (hour, x * 4 + at(y, j), z)

    def dev_z(j):
        return (hour, bus, at(z, j))

    def span(start, size):
        return pl.ds(pl.multiple_of(start, size), size)

    def rows(c):
        return span(c * chunk, chunk)

    def rows_of(c, pos):
        return span(c * chunk + pos * sub, sub)

    def half_rows(c, h):
        return span(c * chunk + h * (chunk // 2), chunk // 2)

    def quarter(q):
        return span(q * QUARTER, QUARTER)

    def copy(kind, j, c):
        own = span(c * sub, sub)
        if kind == OA:
            src = part_a.at[at(x, 2), half_rows(c, j)]
            dst, dev = relay_a.at[j, span(c * (chunk // 2), chunk // 2)], dev_x(j)
        elif kind == DA:
            src = part_a.at[at(x, j), half_rows(c, 1 - j)]
            dst, dev = land_a.at[j, half_rows(c, 1 - j)], dev_x(j)
        elif kind == RA:
            src = part_a.at[at(x, j), half_rows(c, j)]
            dst, dev = land_a.at[j, half_rows(c, j)], dev_x(j)
        elif kind == OB:
            src = part_b.at[pl.ds(2 * j, 2), rows_of(c, at(y, 2))]
            dst, dev = relay_b.at[j, :, own], dev_y(j)
        elif kind == DB:
            src = part_b.at[pl.ds(2 - 2 * j, 2), rows_of(c, at(y, j))]
            dst, dev = land_b.at[j, pl.ds(2 - 2 * j, 2), own], dev_y(j)
        elif kind == RB:
            src = part_b.at[pl.ds(2 * j, 2), rows_of(c, at(y, j))]
            dst, dev = land_b.at[j, pl.ds(2 * j, 2), own], dev_y(j)
        elif kind == S2A:
            src, dst, dev = sum_a.at[rows_of(c, at(y, j))], land2_a.at[j, own], dev_y(j)
        elif kind == S2B:
            src, dst, dev = sum_b.at[at(x, j), own], land2_b.at[j, own], dev_x(j)
        elif kind == AGY:
            src, dst, dev = fg.at[rows_of(c, y)], fg.at[rows_of(c, y)], dev_y(j)
        elif kind == SUMZ:
            src, dst, dev = u.at[rows_of(c, at(z, j))], land_z.at[j, own], dev_z(j)
        elif kind == SUMX:
            src = sum_z.at[own, span(at(x, j) * n_units, n_units)]
            dst, dev = land_x.at[j, own], dev_x(j)
        else:
            src, dst, dev = ob.at[rows_of(c, z)], ob.at[rows_of(c, z)], dev_z(j)
        return pltpu.make_async_remote_copy(
            src_ref=src, dst_ref=dst, send_sem=ssem.at[kind, j, c], recv_sem=rsem.at[kind, j, c],
            device_id=dev, device_id_type=MESH,
        )

    def ways(kind):
        return (2, 0, 1) if kind in WIDE else (0, 1)

    def send(kind, c):
        for j in ways(kind):
            copy(kind, j, c).start()

    def receive(kind, c):
        for j in ways(kind):
            copy(kind, j, c).wait_recv()

    def fetch(q, do):
        last = lines - 3 * QUARTER

        @pl.when(q < 3)
        def _():
            do(pltpu.make_async_copy(ptdf_hbm.at[quarter(q)], p.at[quarter(q)], p_sem.at[q]))

        @pl.when(q == 3)
        def _():
            part = pl.ds(3 * QUARTER, last)
            do(pltpu.make_async_copy(ptdf_hbm.at[part], p.at[part], p_sem.at[3]))

    def g_rows(h):
        return span(h * HALF, HALF)

    def g_copy(j):
        return pltpu.make_async_remote_copy(
            src_ref=g_send.at[j], dst_ref=g.at[x, g_rows(hour)], send_sem=gs_sem.at[j],
            recv_sem=gr_sem.at[j], device_id=dev_x(j), device_id_type=MESH,
        )

    def g_share(j):
        source = at(x, (1, 0, 2)[j])
        return pltpu.make_async_remote_copy(
            src_ref=g.at[source, g_rows(hour)], dst_ref=g.at[source, g_rows(hour)],
            send_sem=cs_sem.at[j], recv_sem=cr_sem.at[j], device_id=sibling, device_id_type=MESH,
        )

    def halo():
        return pltpu.make_async_remote_copy(
            src_ref=gx.at[hours - (hours - 1) * hour], dst_ref=gx.at[(hours + 1) * hour],
            send_sem=halo_sem.at[0], recv_sem=halo_sem.at[1], device_id=sibling, device_id_type=MESH,
        )

    def injection(b):
        per = BLOCK // SCEN
        rest = gx[pl.ds(1 + b * per, per)].reshape(BLOCK, n_units)
        total = -load[span(b * BLOCK, BLOCK), :]
        placed = None
        for _ in range(3):
            head = rest.astype(BF16)
            rest = rest - head.astype(F32)
            term = lax.dot_general(
                head, onehot[...], (((1,), (1,)), ((), ())), preferred_element_type=F32
            )
            placed = term if placed is None else placed + term
        inj[...] = (placed + total).astype(BF16)

    def flows(b, first=False):
        injection(b)
        where = span(b * BLOCK, BLOCK)
        for k in (2, 0, 1, 3):
            q = lax.rem(x + (1, 3, 2, 0)[k], 4)
            if first:
                fetch(q, lambda dma: dma.wait())
            for half in range(2):
                flow = lax.dot_general(
                    inj[...], p[span(q * QUARTER + half * HALF, HALF), :],
                    (((1,), (1,)), ((), ())), preferred_element_type=F32,
                )
                if half == 1:
                    part_b[q, where] = flow.astype(BF16)
                elif k == 3:
                    own_a[where] = flow
                else:
                    part_a[q, where] = flow.astype(BF16)

    def start(c):
        for kind in (OA, OB, DA, DB):
            send(kind, c)

    def relay(c):
        own = span(c * sub, sub)
        for j in range(2):
            copy(OA, j, c).wait_recv()
            q, where = at(x, j), half_rows(c, j)
            there = relay_a[j, span(c * (chunk // 2), chunk // 2), :]
            part_a[q, where, :] = (part_a[q, where, :].astype(F32) + there.astype(F32)).astype(BF16)
            copy(RA, j, c).start()
            copy(OB, j, c).wait_recv()
            where = rows_of(c, at(y, j))
            mine = part_b[2 * j : 2 * j + 2, where, :]
            part_b[2 * j : 2 * j + 2, where, :] = (
                mine.astype(F32) + relay_b[j, :, own, :].astype(F32)
            ).astype(BF16)
            copy(RB, j, c).start()

    def total_a(where):
        return own_a[where, :] + land_a[0, where, :].astype(F32) + land_a[1, where, :].astype(F32)

    def step1(c):
        own = span(c * sub, sub)
        receive(DA, c)
        receive(RA, c)
        sum_a[rows(c), :] = total_a(rows(c)).astype(BF16)
        send(S2A, c)
        receive(DB, c)
        receive(RB, c)
        total = part_b[:, rows_of(c, y), :].astype(F32)
        for j in range(2):
            total = total + land_b[j, :, own, :].astype(F32)
        sum_b[:, own, :] = total.astype(BF16)
        send(S2B, c)

    def step2(c):
        own = span(c * sub, sub)
        per = sub // SCEN
        line = quarter(x)
        mask = jnp.concatenate(
            [
                jnp.broadcast_to(
                    active[pl.ds(c * (4 * per) + y * per + k, 1), line].astype(F32), (SCEN, QUARTER)
                )
                for k in range(per)
            ],
            axis=0,
        )
        scale = 2.0 * wgt[:, line] * mask
        bound = lim[:, line]
        receive(S2A, c)
        total = total_a(rows_of(c, y))
        for j in range(3):
            total = total + land2_a[j, own, :].astype(F32)
        fg[rows_of(c, y), 0:HALF] = (
            scale[:, 0:HALF] * hinge_grad(total, bound[:, 0:HALF])
        ).astype(BF16)
        receive(S2B, c)
        total = part_b[x, rows_of(c, y), :].astype(F32)
        for j in range(2):
            total = total + land_b[j, x, own, :].astype(F32)
        for j in range(3):
            total = total + land2_b[j, own, :].astype(F32)
        fg[rows_of(c, y), HALF:QUARTER] = (
            scale[:, HALF:QUARTER] * hinge_grad(total, bound[:, HALF:QUARTER])
        ).astype(BF16)
        send(AGY, c)

    def step3(c):
        receive(AGY, c)
        for k in range(4):
            u[rows(c), k * n_units : (k + 1) * n_units] = jnp.dot(
                fg[rows(c), :], g[k], preferred_element_type=F32
            )
        send(SUMZ, c)

    def step4(c):
        receive(SUMZ, c)
        own = span(c * sub, sub)
        total = u[rows_of(c, z), :]
        for j in range(3):
            total = total + land_z[j, own, :]
        sum_z[own, :] = total
        send(SUMX, c)

    def step5(c):
        receive(SUMX, c)
        own = span(c * sub, sub)
        total = sum_z[own, span(x * n_units, n_units)]
        for j in range(3):
            total = total + land_x[j, own, :]
        ob[rows_of(c, z), :] = total
        send(AGZ, c)

    def step6(c):
        per = chunk // SCEN
        grid = (per, SCEN, n_units)
        step = gx[pl.ds(c * per + 1, per + 1)] - gx[pl.ds(c * per, per + 1)]
        dual = rw[pl.ds(c * per, per + 1)] * hinge_grad(step, ramp_limit[...][None])
        receive(AGZ, c)
        grad = ob[rows(c), :].reshape(grid) + dual[:-1] - dual[1:]
        out[rows(c), :] = (lev[pl.ds(c * per, per)] * grad).reshape(chunk, n_units)
        for kind in range(KINDS):
            for j in ways(kind):
                copy(kind, j, c).wait_send()

    locals_in = [
        pltpu.make_async_copy(src, dst, in_sem.at[n])
        for n, (src, dst) in enumerate(
            [
                (commit_hbm, commit),
                (units_hbm, units),
                (load_hbm, load),
                (active_hbm, active.at[:, pl.ds(0, lines)]),
                (ramp_hbm, ramp),
            ]
        )
    ]
    for dma in locals_in[:3]:
        dma.start()
    for k in (2, 0, 1, 3):
        fetch(lax.rem(x + (1, 3, 2, 0)[k], 4), lambda dma: dma.start())
    for dma in locals_in[3:]:
        dma.start()
    barrier = pltpu.get_barrier_semaphore()
    for j in range(3):
        for dev in (dev_x(j), dev_y(j), dev_z(j)):
            pl.semaphore_signal(barrier, inc=1, device_id=dev, device_id_type=MESH)
    pl.semaphore_signal(barrier, inc=1, device_id=sibling, device_id_type=MESH)

    fill = 4 * QUARTER - lines
    p[lines:, :] = jnp.zeros((fill, nodes), BF16)
    active[:, lines:] = jnp.zeros((hours, fill), jnp.int32)
    lim[:, lines:] = jnp.zeros((1, fill), F32)
    wgt[:, lines:] = jnp.zeros((1, fill), F32)
    lim[:, :lines] = limit[...]
    wgt[:, :lines] = weight[...]
    onehot[...] = (
        lax.broadcasted_iota(jnp.int32, onehot.shape, 0) == node[...] - bus * nodes
    ).astype(F32).astype(BF16)
    gx[(hours + 1) * hour] = jnp.zeros((SCEN, n_units), F32)
    locals_in[0].wait()
    locals_in[1].wait()

    def generate(k, carry):
        row = commit[pl.ds(k, 1), :]
        value = jnp.zeros((1, n_units), F32)
        for n in range(levels.shape[0]):
            value = value + jnp.where(row == n, levels[n], 0.0)
        value = jnp.broadcast_to(value, (SCEN, n_units))
        lev[k] = value
        gx[k + 1] = value * units[k]
        return carry

    lax.fori_loop(0, hours, generate, 0)
    locals_in[2].wait()
    flows(0, first=True)
    pl.semaphore_wait(barrier, 10)
    start(0)
    halo().start()
    for j in range(3):
        g_send[j] = jnp.dot(
            p[span(at(x, j) * QUARTER + hour * HALF, HALF), :], onehot[...],
            preferred_element_type=F32,
        ).astype(BF16)
        g_copy(j).start()
    g[x] = jnp.dot(p[quarter(x), :], onehot[...], preferred_element_type=F32).astype(BF16)
    locals_in[3].wait()
    locals_in[4].wait()

    def ramps(k, carry):
        index = lax.rem(hour * hours + k, 2 * hours)
        inner = (index != 0).astype(F32)
        row = 2.0 * ramp_weight[...] * (ramp[pl.ds(index, 1), :].astype(F32) * inner)
        rw[k] = jnp.broadcast_to(row, (SCEN, n_units))
        return carry

    lax.fori_loop(0, hours + 1, ramps, 0)
    halo().wait()

    stages = [(flows, 0), (step6, 7), (step5, 6), (step4, 5), (step3, 4), (step2, 3), (step1, 2), (relay, 1)]
    per = BLOCK // chunk

    def body(i, carry):
        @pl.when(i < CHUNKS)
        def _():
            if per == 1:
                flows(i)
            else:
                @pl.when(lax.rem(i, per) == 0)
                def _():
                    flows(i // per)
            start(i)

        for stage, lag in stages[1:]:
            if stage is step3:
                @pl.when(i == lag)
                def _():
                    for j in range(3):
                        g_share(j).wait_recv()

            @pl.when((i >= lag) & (i < CHUNKS + lag))
            def _():
                stage(i - lag)

            if stage is step2:
                @pl.when(i == lag)
                def _():
                    for j in range(3):
                        g_copy(j).wait_recv()
                        g_share(j).start()

        return carry

    lax.fori_loop(1, CHUNKS + 7, body, 0)
    for j in range(3):
        g_copy(j).wait_send()
        g_share(j).wait_send()


def body(
    ptdf, units_out, load, unit_node, commit_index, relax_levels,
    line_active, line_limit, line_weight, ramp_active, ramp_limit, ramp_weight,
):
    hours, scen, units = units_out.shape
    lines, nodes = ptdf.shape
    columns = hours * scen
    vmem = pl.BlockSpec(memory_space=pltpu.VMEM)
    smem = pl.BlockSpec(memory_space=pltpu.SMEM)
    anywhere = pl.BlockSpec(memory_space=pl.ANY)
    dma = pltpu.SemaphoreType.DMA
    all_lines = 4 * QUARTER
    own = columns // 4
    grad = pl.pallas_call(
        kernel,
        out_shape=jax.ShapeDtypeStruct((columns, units), F32),
        in_specs=[smem] + [anywhere] * 6 + [vmem] * 5,
        out_specs=vmem,
        scratch_shapes=[
            pltpu.VMEM((all_lines, nodes), BF16),
            pltpu.VMEM((columns, nodes), F32),
            pltpu.VMEM((hours, scen, units), F32),
            pltpu.VMEM((hours, units), jnp.int32),
            pltpu.VMEM((hours, all_lines), jnp.int32),
            pltpu.VMEM((2 * hours, units), jnp.int32),
            pltpu.VMEM((hours, scen, units), F32),
            pltpu.VMEM((hours + 2, scen, units), F32),
            pltpu.VMEM((hours + 1, scen, units), F32),
            pltpu.VMEM((1, all_lines), F32),
            pltpu.VMEM((1, all_lines), F32),
            pltpu.VMEM((BLOCK, nodes), BF16),
            pltpu.VMEM((4, columns, HALF), BF16),
            pltpu.VMEM((4, columns, HALF), BF16),
            pltpu.VMEM((columns, HALF), F32),
            pltpu.VMEM((2, columns // 2, HALF), BF16),
            pltpu.VMEM((2, 2, own, HALF), BF16),
            pltpu.VMEM((2, columns, HALF), BF16),
            pltpu.VMEM((2, 4, own, HALF), BF16),
            pltpu.VMEM((columns, HALF), BF16),
            pltpu.VMEM((4, own, HALF), BF16),
            pltpu.VMEM((3, own, HALF), BF16),
            pltpu.VMEM((3, own, HALF), BF16),
            pltpu.VMEM((columns, QUARTER), BF16),
            pltpu.VMEM((columns, 4 * units), F32),
            pltpu.VMEM((3, own, 4 * units), F32),
            pltpu.VMEM((own, 4 * units), F32),
            pltpu.VMEM((3, own, units), F32),
            pltpu.VMEM((columns, units), F32),
            pltpu.VMEM((nodes, units), BF16),
            pltpu.VMEM((3, HALF, units), BF16),
            pltpu.VMEM((4, QUARTER, units), BF16),
            dma((4,)),
            dma((5,)),
            dma((KINDS, 3, CHUNKS)),
            dma((KINDS, 3, CHUNKS)),
            dma((3,)),
            dma((3,)),
            dma((3,)),
            dma((3,)),
            dma((2,)),
        ],
        compiler_params=pltpu.CompilerParams(
            collective_id=0, has_side_effects=True, vmem_limit_bytes=62 << 20
        ),
    )(
        relax_levels, ptdf, load.reshape(columns, nodes), units_out, commit_index, line_active,
        ramp_active, unit_node[None, :], line_limit[None, :], line_weight[None, :],
        ramp_limit[None, :], ramp_weight[None, :],
    )
    return grad.reshape(hours, scen, units)


def solution(mesh):
    return jax.shard_map(
        body,
        mesh=mesh,
        in_specs=(
            P("line", "bus"),
            P("hour", None, "bus"),
            P("hour", None, "bus"),
            P("bus"),
            P("hour", "bus"),
            P(),
            P("hour", "line"),
            P("line"),
            P("line"),
            P(None, "bus"),
            P("bus"),
            P("bus"),
        ),
        out_specs=P("hour", None, "bus"),
        check_vma=False,
    )
```

time: 147 us -> 126 us (0.86)
  Pallas kernels: 127 us -> 121 us
  other arithmetic: 5.51 us -> 0 us
  matrix products: 4.7 us -> 0 us
  starting transfers between devices: 4.32 us -> 0 us
    pallas_call x1, Pallas kernels: 127 us -> 121 us  [body(): pl.pallas_call(kernel, out_shape=jax.ShapeDtypeStruct((columns, units), F...]
    dot_general x1 -> x0, matrix products: 4.7 us -> none  [body(): jnp.dot(generation.reshape(columns, units_dev), onehot, precision=lax.Pre...]
    mul x7 -> x0, other arithmetic: 4.48 us -> none  [the longest x1 2.14 us: body(): return unit_level[:, None, :] * (unit_grad + ramp_dual[:-1] - ramp_dual[1:])]
    ppermute x2 -> x0, starting transfers between devices: 4.32 us -> none  [the longest x1 3.03 us: body(): low = lax.ppermute(generation[-1:], 'hour', [(0, 1)])]
    reshape x2 -> x0, local copies, waits for them, and re-layouts: 2.92 us -> none  [the longest x1 1.88 us: body(): line_active.reshape(CHUNKS, 4, sub_hours, lines_dev)]
    broadcast_in_dim x1 -> x2, local copies, waits for them, and re-layouts: 0.6 us -> 2.69 us  [the longest x1 1.35 us: body(): line_limit[None, :]]
    unnamed x10 -> x1, local copies, waits for them, and re-layouts: 0.03 us -> 2.06 us
  transfers between devices with their start and end apart: 2 -> 0, of which waited for: 0 -> 0; matrix products, arithmetic and copies ran while one was open for 7% -> 0% of each run, Pallas kernels for 87% -> 0%
where the time goes in v2:
time: 126 us
  Pallas kernels  121 us (96%)
  local copies, waits for them, and re-layouts  4.75 us (4%)
    pallas_call x1, Pallas kernels, body(): pl.pallas_call(kernel, out_shape=jax.ShapeDtypeStruct((columns, units), F...  121 us

profile of v2, /device:TPU:0, one launch (start us, length us, event | category | flops | bytes accessed | tf_op | source)
XLA Modules:
  0.0 125.9 jit_solution(16574022228875965673)
XLA Ops:
  0.0 1.3 %broadcast_in_dim.16.limit = f32[1,4992]{1,0:T(1,128)} reshape(f32[4992]{0:T(1024)} %param.19) | data formatting | bytes 39936 | tf_op jit(solution)/shard_map/broadcast_in_dim | solution.py:478
  1.3 1.3 %broadcast_in_dim.17.weight = f32[1,4992]{1,0:T(1,128)} reshape(f32[4992]{0:T(1024)} %param.20) | data formatting | bytes 39936 | tf_op jit(solution)/shard_map/broadcast_in_dim | solution.py:478
  2.7 121.2 %shard_map.118 = f32[768,256]{1,0:T(8,128)} custom-call(f32[4]{0:T(128)} %levels.1, bf16[4992,1024]{1,0:T(8,128)(2,1)} %ptdf_hbm.1, f32[768,1024]{1,0:T(8,128)} %bitcast.6, f32[96,8,256]{2,1,0:T(8,128)} %units_hbm.1, s32[96,256]{1,0:T(8,128)} %commit_hbm.1, s32[96,4992]{1,0:T(8,128)} %active_hbm.1, s32[192,256]{1,0:T(8,128)} %ramp_hbm.1, s32[1,256]{1,0:T(1,128)} %bitcast.7, ...), custom_call_target="tpu_custom_call" | custom-call | tf_op jit(solution)/shard_map/pallas_call | solution.py:425
  123.9 2.1 %copy.14 = f32[96,8,256]{2,1,0:T(8,128)} copy(f32[96,8,256]{2,1,0:T(8,128)} %bitcast.5) | data formatting | bytes 1572864

commit v3 on v2

v3 whole, which is shorter than its diff:
```python
import jax
import jax.numpy as jnp
from jax import lax
from jax.experimental import pallas as pl
from jax.experimental.pallas import tpu as pltpu
from jax.sharding import PartitionSpec as P

MESH = pl.DeviceIdType.MESH
F32 = jnp.float32
BF16 = jnp.bfloat16

CHUNKS = 6
HALF = 640
QUARTER = 2 * HALF
SCEN = 8
OA, OB, TA, TB, S2A, S2B, AGY, SUMZ, SUMX, AGZ = range(10)
KINDS = 10
ORDER = (("F", 0), ("6", 20), ("1", 4), ("3", 8), ("5", 15), ("R", 2), ("4", 12), ("2", 5))


def hinge_grad(values, limits):
    return jnp.maximum(values - limits, 0.0) - jnp.maximum(-values - limits, 0.0)


def kernel(
    levels, ptdf_hbm, load_hbm, units_hbm, commit_hbm, active_hbm, ramp_hbm, limit_hbm, weight_hbm,
    node, ramp_limit, ramp_weight, out,
    p, load, units, commit, active, ramp, lev, gx, rw, lim, wgt, inj,
    part_a, part_b, own_a, relay_a, relay_b, land_a, land_b, sum_a, sum_b, land2_a, land2_b,
    fg, u, u_send, land_z, sum_z, land_x, ob, onehot, g_send, g,
    p_sem, in_sem, ssem, rsem, g_sem, halo_sem,
):
    columns, nodes = load.shape
    hours = columns // SCEN
    lines = ptdf_hbm.shape[0]
    n_units = node.shape[1]
    chunk = columns // CHUNKS
    sub = chunk // 4
    hour = lax.axis_index("hour")
    bus = lax.axis_index("bus")
    z = lax.axis_index("line")
    x = bus // 4
    y = bus % 4
    sibling = (1 - hour, bus, z)

    def at(pos, j):
        return lax.rem(pos + (1, 3, 2)[j], 4)

    def dev_x(j):
        return (hour, at(x, j) * 4 + y, z)

    def dev_y(j):
        return (hour, x * 4 + at(y, j), z)

    def dev_z(j):
        return (hour, bus, at(z, j))

    def span(start, size):
        return pl.ds(pl.multiple_of(start, size), size)

    def rows(c):
        return span(c * chunk, chunk)

    def own(c):
        return span(c * sub, sub)

    def rows_of(c, pos):
        return span(c * chunk + pos * sub, sub)

    def half_rows(c, h):
        return span(c * chunk + h * (chunk // 2), chunk // 2)

    def own_rows(c, times):
        return pl.ds(pl.multiple_of(c * chunk, chunk), times * sub)

    def over_rows(start, size, step, work):
        @pl.loop(0, size // step)
        def _(k):
            work(span(start + k * step, step))

    def quarter(q):
        return pl.ds(pl.multiple_of(q * QUARTER, QUARTER), QUARTER)

    def unit_lanes(pos):
        return pl.ds(pl.multiple_of(pos * n_units, n_units), n_units)

    def push(src, dst, send_sem, recv_sem, dev):
        pltpu.make_async_remote_copy(
            src_ref=src, dst_ref=dst, send_sem=send_sem, recv_sem=recv_sem,
            device_id=dev, device_id_type=MESH,
        ).start()

    def take(ref, sem):
        pltpu.make_async_copy(ref, ref, sem).wait()

    def receive(kind, c, ref):
        take(ref, rsem.at[kind, c])

    def fetch(q, do):
        last = lines - 3 * QUARTER

        @pl.when(q < 3)
        def _():
            do(pltpu.make_async_copy(ptdf_hbm.at[quarter(q)], p.at[quarter(q)], p_sem.at[q]))

        @pl.when(q == 3)
        def _():
            part = pl.ds(3 * QUARTER, last)
            do(pltpu.make_async_copy(ptdf_hbm.at[part], p.at[part], p_sem.at[3]))

    def injection(c):
        per = chunk // SCEN
        rest = gx[pl.ds(1 + c * per, per)].reshape(chunk, n_units)
        placed = None
        for _ in range(3):
            head = rest.astype(BF16)
            rest = rest - head.astype(F32)
            term = lax.dot_general(
                head, onehot[...], (((1,), (1,)), ((), ())), preferred_element_type=F32
            )
            placed = term if placed is None else placed + term
        inj[...] = (placed - load[rows(c), :]).astype(BF16)

    def product(q, half):
        where = pl.ds(pl.multiple_of(q * QUARTER + half * HALF, HALF), HALF)
        return lax.dot_general(
            inj[...], p[where, :], (((1,), (1,)), ((), ())), preferred_element_type=F32
        )

    def forward(c):
        injection(c)

        @pl.loop(0, 4)
        def _(k):
            q = lax.rem(x + 2 + k, 4)

            @pl.when(c == 0)
            def _():
                fetch(q, lambda dma: dma.wait())

            flow = product(q, 0)
            part_a[q, rows(c)] = flow.astype(BF16)

            @pl.when(k == 2)
            def _():
                own_a[rows(c)] = flow

            part_b[q, rows(c)] = product(q, 1).astype(BF16)

        @pl.when(c == 0)
        def _():
            pl.semaphore_wait(pltpu.get_barrier_semaphore(), 10)

        for j in range(2):
            push(part_a.at[at(x, 2), half_rows(c, j)], relay_a.at[half_rows(c, j)],
                 ssem.at[OA], rsem.at[OA, c], dev_x(j))
            pair = pl.ds(2 * j, 2)
            push(part_b.at[pair, rows_of(c, at(y, 2))], relay_b.at[pair, own(c)],
                 ssem.at[OB], rsem.at[OB, c], dev_y(j))
        for j in range(2):
            half = half_rows(c, 1 - j)
            push(part_a.at[at(x, j), half], land_a.at[j, half], ssem.at[OA], rsem.at[TA, c], dev_x(j))
            pair = pl.ds(2 - 2 * j, 2)
            push(part_b.at[pair, rows_of(c, at(y, j))], land_b.at[j, pair, own(c)],
                 ssem.at[OB], rsem.at[TB, c], dev_y(j))

    def relay(c):
        receive(OA, c, relay_a.at[rows(c)])
        for j in range(2):
            q = at(x, j)

            def add_a(where):
                part_a[q, where, :] = (
                    part_a[q, where, :].astype(F32) + relay_a[where, :].astype(F32)
                ).astype(BF16)

            over_rows(c * chunk + j * (chunk // 2), chunk // 2, 16, add_a)
            half = half_rows(c, j)
            push(part_a.at[q, half], land_a.at[j, half], ssem.at[OA], rsem.at[TA, c], dev_x(j))
        receive(OB, c, relay_b.at[:, own(c)])
        for j in range(2):
            where = rows_of(c, at(y, j))

            @pl.loop(2 * j, 2 * j + 2)
            def _(q):
                part_b[q, where, :] = (
                    part_b[q, where, :].astype(F32) + relay_b[q, own(c), :].astype(F32)
                ).astype(BF16)

            pair = pl.ds(2 * j, 2)
            push(part_b.at[pair, where], land_b.at[j, pair, own(c)],
                 ssem.at[OB], rsem.at[TB, c], dev_y(j))

    def total_a(where):
        return own_a[where, :] + land_a[0, where, :].astype(F32) + land_a[1, where, :].astype(F32)

    def total_b(c, q):
        total = part_b[q, rows_of(c, y), :].astype(F32)
        for j in range(2):
            total = total + land_b[j, q, own(c), :].astype(F32)
        return total

    def step1(c):
        receive(TA, c, land_a.at[:, rows(c)])

        def add_a(where):
            sum_a[where, :] = total_a(where).astype(BF16)

        over_rows(c * chunk, chunk, 16, add_a)
        for j in (2, 0, 1):
            push(sum_a.at[rows_of(c, at(y, j))], land2_a.at[j, own(c)],
                 ssem.at[S2A], rsem.at[S2A, c], dev_y(j))
        receive(TB, c, land_b.at[:, :, own(c)])

        @pl.loop(0, 4)
        def _(q):
            sum_b[q, own(c), :] = total_b(c, q).astype(BF16)

        for j in (2, 0, 1):
            push(sum_b.at[at(x, j), own(c)], land2_b.at[j, own(c)],
                 ssem.at[S2B], rsem.at[S2B, c], dev_x(j))

    def step2(c):
        per = sub // SCEN
        line = quarter(x)
        mask = jnp.concatenate(
            [
                jnp.broadcast_to(
                    active[pl.ds((c * 4 + y) * per + k, 1), line].astype(F32), (SCEN, QUARTER)
                )
                for k in range(per)
            ],
            axis=0,
        )
        scale = 2.0 * wgt[:, line] * mask
        bound = lim[:, line]
        where = rows_of(c, y)
        receive(S2A, c, land2_a.at[:, own(c)])
        total = total_a(where)
        for j in range(3):
            total = total + land2_a[j, own(c), :].astype(F32)
        fg[where, 0:HALF] = (scale[:, 0:HALF] * hinge_grad(total, bound[:, 0:HALF])).astype(BF16)
        receive(S2B, c, land2_b.at[:, own(c)])
        total = total_b(c, x)
        for j in range(3):
            total = total + land2_b[j, own(c), :].astype(F32)
        fg[where, HALF:QUARTER] = (
            scale[:, HALF:QUARTER] * hinge_grad(total, bound[:, HALF:QUARTER])
        ).astype(BF16)
        for j in (2, 0, 1):
            push(fg.at[where], fg.at[where], ssem.at[AGY], rsem.at[AGY, c], dev_y(j))

    def step3(c):
        @pl.when(c == 0)
        def _():
            take(g_send, g_sem.at[3])

        receive(AGY, c, fg.at[own_rows(c, 3)])

        @pl.loop(0, 4)
        def _(k):
            grad = jnp.dot(fg[rows(c), :], g[k], preferred_element_type=F32)
            u[rows(c), unit_lanes(k)] = grad
            u_send[rows(c), unit_lanes(k)] = grad.astype(BF16)

        for j in (2, 0, 1):
            push(u_send.at[rows_of(c, at(z, j))], land_z.at[j, own(c)],
                 ssem.at[SUMZ], rsem.at[SUMZ, c], dev_z(j))

    def step4(c):
        receive(SUMZ, c, land_z.at[:, own(c)])

        @pl.loop(0, 4)
        def _(k):
            total = u[rows_of(c, z), unit_lanes(k)]
            for j in range(3):
                total = total + land_z[j, own(c), unit_lanes(k)].astype(F32)
            sum_z[own(c), unit_lanes(k)] = total

        for j in (2, 0, 1):
            push(sum_z.at[own(c), unit_lanes(at(x, j))], land_x.at[j, own(c)],
                 ssem.at[SUMX], rsem.at[SUMX, c], dev_x(j))

    def step5(c):
        receive(SUMX, c, land_x.at[:, own(c)])
        total = sum_z[own(c), unit_lanes(x)]
        for j in range(3):
            total = total + land_x[j, own(c), :]
        where = rows_of(c, z)
        ob[where, :] = total
        for j in (2, 0, 1):
            push(ob.at[where], ob.at[where], ssem.at[AGZ], rsem.at[AGZ, c], dev_z(j))

    def step6(c):
        receive(AGZ, c, ob.at[own_rows(c, 3)])
        per = chunk // SCEN
        bound = ramp_limit[...][None]

        @pl.loop(0, per // 4)
        def _(k):
            h = c * per + k * 4
            step = gx[pl.ds(h + 1, 5)] - gx[pl.ds(h, 5)]
            dual = rw[pl.ds(h, 5)] * hinge_grad(step, bound)
            where = span(h * SCEN, 4 * SCEN)
            grad = ob[where, :].reshape(4, SCEN, n_units) + dual[:-1] - dual[1:]
            out[where, :] = (lev[pl.ds(h, 4)] * grad).reshape(4 * SCEN, n_units)

    def g_rows(h):
        return pl.ds(pl.multiple_of(h * HALF, HALF), HALF)

    def send_factor(j):
        where = pl.ds(pl.multiple_of(at(x, j) * QUARTER + hour * HALF, HALF), HALF)
        g_send[j] = jnp.dot(p[where, :], onehot[...], preferred_element_type=F32).astype(BF16)
        push(g_send.at[j], g.at[x, g_rows(hour)], g_sem.at[0], g_sem.at[1], dev_x(j))

    def own_factor():
        g[x] = jnp.dot(p[quarter(x), :], onehot[...], preferred_element_type=F32).astype(BF16)
        locals_in[3].wait()
        locals_in[4].wait()

        def ramps(k, carry):
            index = lax.rem(hour * hours + k, 2 * hours)
            inner = (index != 0).astype(F32)
            row = 2.0 * ramp_weight[...] * (ramp[pl.ds(index, 1), :].astype(F32) * inner)
            rw[k] = jnp.broadcast_to(row, (SCEN, n_units))
            return carry

        lax.fori_loop(0, hours + 1, ramps, 0)
        halo().wait()

    def share_factors():
        take(g_send, g_sem.at[1])
        for j in range(3):
            part = g.at[at(x, j), g_rows(hour)]
            push(part, part, g_sem.at[2], g_sem.at[3], sibling)

    def halo():
        return pltpu.make_async_remote_copy(
            src_ref=gx.at[hours - (hours - 1) * hour], dst_ref=gx.at[(hours + 1) * hour],
            send_sem=halo_sem.at[0], recv_sem=halo_sem.at[1], device_id=sibling, device_id_type=MESH,
        )

    locals_in = [
        pltpu.make_async_copy(src, dst, in_sem.at[n])
        for n, (src, dst) in enumerate(
            [
                (commit_hbm, commit),
                (units_hbm, units),
                (load_hbm, load),
                (active_hbm, active.at[:, pl.ds(0, lines)]),
                (ramp_hbm, ramp),
                (limit_hbm, lim.at[0, pl.ds(0, lines)]),
                (weight_hbm, wgt.at[0, pl.ds(0, lines)]),
            ]
        )
    ]
    for dma in locals_in[:2]:
        dma.start()
    for k in range(4):
        fetch(lax.rem(x + (2, 1, 3, 0)[k], 4), lambda dma: dma.start())
        if k == 0:
            locals_in[2].start()
    for dma in locals_in[3:]:
        dma.start()
    barrier = pltpu.get_barrier_semaphore()
    for j in range(3):
        for dev in (dev_x(j), dev_y(j), dev_z(j)):
            pl.semaphore_signal(barrier, inc=1, device_id=dev, device_id_type=MESH)
    pl.semaphore_signal(barrier, inc=1, device_id=sibling, device_id_type=MESH)

    fill = 4 * QUARTER - lines
    p[lines:, :] = jnp.zeros((fill, nodes), BF16)
    active[:, lines:] = jnp.zeros((hours, fill), jnp.int32)
    lim[:, lines:] = jnp.zeros((1, fill), F32)
    wgt[:, lines:] = jnp.zeros((1, fill), F32)
    onehot[...] = (
        lax.broadcasted_iota(jnp.int32, onehot.shape, 0) == node[...] - bus * nodes
    ).astype(F32).astype(BF16)
    gx[(hours + 1) * hour] = jnp.zeros((SCEN, n_units), F32)
    locals_in[0].wait()
    locals_in[1].wait()

    def generate(k, carry):
        row = commit[pl.ds(k, 1), :]
        value = jnp.zeros((1, n_units), F32)
        for n in range(levels.shape[0]):
            value = value + jnp.where(row == n, levels[n], 0.0)
        value = jnp.broadcast_to(value, (SCEN, n_units))
        lev[k] = value
        gx[k + 1] = value * units[k]
        return carry

    lax.fori_loop(0, hours, generate, 0)
    locals_in[2].wait()

    steps = dict(zip("FR123456", (forward, relay, step1, step2, step3, step4, step5, step6)))

    def iteration(i, carry):
        for name, lag in ORDER:
            if name == "2":
                @pl.when(i == lag)
                def _():
                    locals_in[5].wait()
                    locals_in[6].wait()
            if name == "3":
                @pl.when(i == lag)
                def _():
                    share_factors()

            @pl.when((i >= lag) & (i < CHUNKS + lag))
            def _():
                steps[name](i - lag)

            if name == "F":
                @pl.when(i == 0)
                def _():
                    halo().start()
                    for j in (2, 0, 1):
                        send_factor(j)
                    own_factor()

        return carry

    lax.fori_loop(0, CHUNKS + max(lag for _, lag in ORDER), iteration, 0)
    take(part_a.at[pl.ds(0, 3)], ssem.at[OA])
    take(part_b.at[pl.ds(0, 3)], ssem.at[OB])
    take(land2_a, ssem.at[S2A])
    take(land2_b, ssem.at[S2B])
    take(fg.at[pl.ds(0, 3 * (columns // 4))], ssem.at[AGY])
    take(land_z, ssem.at[SUMZ])
    take(land_x, ssem.at[SUMX])
    take(land_x, ssem.at[AGZ])
    take(g_send, g_sem.at[0])
    take(g_send, g_sem.at[2])


def body(
    ptdf, units_out, load, unit_node, commit_index, relax_levels,
    line_active, line_limit, line_weight, ramp_active, ramp_limit, ramp_weight,
):
    hours, scen, units = units_out.shape
    lines, nodes = ptdf.shape
    columns = hours * scen
    vmem = pl.BlockSpec(memory_space=pltpu.VMEM)
    smem = pl.BlockSpec(memory_space=pltpu.SMEM)
    anywhere = pl.BlockSpec(memory_space=pl.ANY)
    dma = pltpu.SemaphoreType.DMA
    all_lines = 4 * QUARTER
    own = columns // 4
    grad = pl.pallas_call(
        kernel,
        out_shape=jax.ShapeDtypeStruct((columns, units), F32),
        in_specs=[smem] + [anywhere] * 8 + [vmem] * 3,
        out_specs=vmem,
        scratch_shapes=[
            pltpu.VMEM((all_lines, nodes), BF16),
            pltpu.VMEM((columns, nodes), F32),
            pltpu.VMEM((hours, scen, units), F32),
            pltpu.VMEM((hours, units), jnp.int32),
            pltpu.VMEM((hours, all_lines), jnp.int32),
            pltpu.VMEM((2 * hours, units), jnp.int32),
            pltpu.VMEM((hours, scen, units), F32),
            pltpu.VMEM((hours + 2, scen, units), F32),
            pltpu.VMEM((hours + 1, scen, units), F32),
            pltpu.VMEM((1, all_lines), F32),
            pltpu.VMEM((1, all_lines), F32),
            pltpu.VMEM((columns // CHUNKS, nodes), BF16),
            pltpu.VMEM((4, columns, HALF), BF16),
            pltpu.VMEM((4, columns, HALF), BF16),
            pltpu.VMEM((columns, HALF), F32),
            pltpu.VMEM((columns, HALF), BF16),
            pltpu.VMEM((4, own, HALF), BF16),
            pltpu.VMEM((2, columns, HALF), BF16),
            pltpu.VMEM((2, 4, own, HALF), BF16),
            pltpu.VMEM((columns, HALF), BF16),
            pltpu.VMEM((4, own, HALF), BF16),
            pltpu.VMEM((3, own, HALF), BF16),
            pltpu.VMEM((3, own, HALF), BF16),
            pltpu.VMEM((columns, QUARTER), BF16),
            pltpu.VMEM((columns, 4 * units), F32),
            pltpu.VMEM((columns, 4 * units), BF16),
            pltpu.VMEM((3, own, 4 * units), BF16),
            pltpu.VMEM((own, 4 * units), F32),
            pltpu.VMEM((3, own, units), F32),
            pltpu.VMEM((columns, units), F32),
            pltpu.VMEM((nodes, units), BF16),
            pltpu.VMEM((3, HALF, units), BF16),
            pltpu.VMEM((4, QUARTER, units), BF16),
            dma((4,)),
            dma((7,)),
            dma((KINDS,)),
            dma((KINDS, CHUNKS)),
            dma((4,)),
            dma((2,)),
        ],
        compiler_params=pltpu.CompilerParams(
            collective_id=0, has_side_effects=True, vmem_limit_bytes=62 << 20
        ),
    )(
        relax_levels, ptdf, load.reshape(columns, nodes), units_out, commit_index, line_active,
        ramp_active, line_limit, line_weight, unit_node[None, :], ramp_limit[None, :],
        ramp_weight[None, :],
    )
    return grad.reshape(hours, scen, units)


def solution(mesh):
    return jax.shard_map(
        body,
        mesh=mesh,
        in_specs=(
            P("line", "bus"),
            P("hour", None, "bus"),
            P("hour", None, "bus"),
            P("bus"),
            P("hour", "bus"),
            P(),
            P("hour", "line"),
            P("line"),
            P("line"),
            P(None, "bus"),
            P("bus"),
            P("bus"),
        ),
        out_specs=P("hour", None, "bus"),
        check_vma=False,
    )
```

time: 126 us -> 112 us (0.89)
  Pallas kernels: 121 us -> 110 us
  local copies, waits for them, and re-layouts: 4.75 us -> 2.06 us
    pallas_call x1, Pallas kernels: 121 us -> 110 us  [body(): pl.pallas_call(kernel, out_shape=jax.ShapeDtypeStruct((columns, units), F...]
    broadcast_in_dim x2 -> x0, local copies, waits for them, and re-layouts: 2.69 us -> none  [the longest x1 1.35 us: body(): line_limit[None, :]]
where the time goes in v3:
time: 112 us
  Pallas kernels  110 us (98%)
  local copies, waits for them, and re-layouts  2.06 us (2%)
    pallas_call x1, Pallas kernels, body(): pl.pallas_call(kernel, out_shape=jax.ShapeDtypeStruct((columns, units), F...  110 us

profile of v3, /device:TPU:0, one launch (start us, length us, event | category | flops | bytes accessed | tf_op | source)
XLA Modules:
  0.0 111.7 jit_solution(2775594520853684471)
XLA Ops:
  0.0 109.6 %shard_map.118 = f32[768,256]{1,0:T(8,128)} custom-call(f32[4]{0:T(128)} %levels.1, bf16[4992,1024]{1,0:T(8,128)(2,1)} %ptdf_hbm.1, f32[768,1024]{1,0:T(8,128)} %bitcast.6, f32[96,8,256]{2,1,0:T(8,128)} %units_hbm.1, s32[96,256]{1,0:T(8,128)} %commit_hbm.1, s32[96,4992]{1,0:T(8,128)} %active_hbm.1, s32[192,256]{1,0:T(8,128)} %ramp_hbm.1, f32[4992]{0:T(1024)} %limit_hbm.1, ...), custom_call_target="tpu_custom_call" | custom-call | tf_op jit(solution)/shard_map/pallas_call | solution.py:450
  109.6 2.1 %copy.14 = f32[96,8,256]{2,1,0:T(8,128)} copy(f32[96,8,256]{2,1,0:T(8,128)} %bitcast.5) | data formatting | bytes 1572864

commit v4 on v3

--- a/solution.py
+++ b/solution.py
@@ -10,12 +10,16 @@
 BF16 = jnp.bfloat16
 
 CHUNKS = 6
-HALF = 640
-QUARTER = 2 * HALF
+TOGETHER = 2
+QUARTER = 1280
+SIDE_A = 512
+SIDE_B = QUARTER - SIDE_A
+HALF = QUARTER // 2
 SCEN = 8
-OA, OB, TA, TB, S2A, S2B, AGY, SUMZ, SUMX, AGZ = range(10)
-KINDS = 10
-ORDER = (("F", 0), ("6", 20), ("1", 4), ("3", 8), ("5", 15), ("R", 2), ("4", 12), ("2", 5))
+OA, OB, TA, TB, S2A, S2B, AGY, AGR, SUMZ, SUMX, AGZ = range(11)
+KINDS = 11
+ORDER = (("F", 0), ("Y", 6), ("2", 5), ("5", 10), ("4", 8), ("1", 3), ("3", 6), ("R", 1), ("6", 11))
+FACTORS = (1, 3, 2, 5)
 
 
 def hinge_grad(values, limits):
@@ -36,6 +40,7 @@
     n_units = node.shape[1]
     chunk = columns // CHUNKS
     sub = chunk // 4
+    block = chunk * TOGETHER
     hour = lax.axis_index("hour")
     bus = lax.axis_index("bus")
     z = lax.axis_index("line")
@@ -109,8 +114,8 @@
             do(pltpu.make_async_copy(ptdf_hbm.at[part], p.at[part], p_sem.at[3]))
 
     def injection(c):
-        per = chunk // SCEN
-        rest = gx[pl.ds(1 + c * per, per)].reshape(chunk, n_units)
+        per = block // SCEN
+        rest = gx[pl.ds(1 + c * (chunk // SCEN), per)].reshape(block, n_units)
         placed = None
         for _ in range(3):
             head = rest.astype(BF16)
@@ -119,16 +124,36 @@
                 head, onehot[...], (((1,), (1,)), ((), ())), preferred_element_type=F32
             )
             placed = term if placed is None else placed + term
-        inj[...] = (placed - load[rows(c), :]).astype(BF16)
-
-    def product(q, half):
-        where = pl.ds(pl.multiple_of(q * QUARTER + half * HALF, HALF), HALF)
+        where = pl.ds(pl.multiple_of(c * chunk, chunk), block)
+        inj[...] = (placed - load[where, :]).astype(BF16)
+
+    def product(start, size):
+        where = pl.ds(pl.multiple_of(start, 128), size)
         return lax.dot_general(
             inj[...], p[where, :], (((1,), (1,)), ((), ())), preferred_element_type=F32
         )
 
-    def forward(c):
+    def send_far_a(c):
+        for j in range(2):
+            push(part_a.at[at(x, 2), half_rows(c, j)], relay_a.at[half_rows(c, j)],
+                 ssem.at[OA], rsem.at[OA, c], dev_x(j))
+
+    def send_near_a(c, j):
+        half = half_rows(c, 1 - j)
+        push(part_a.at[at(x, j), half], land_a.at[j, half], ssem.at[OA], rsem.at[TA, c], dev_x(j))
+
+    def send_b(c, q):
+        side = q // 2
+        far = lax.rem(y + 1 + 2 * side, 4)
+        push(part_b.at[q, rows_of(c, at(y, 2))], relay_b.at[q, own(c)],
+             ssem.at[OB], rsem.at[OB, c], (hour, x * 4 + far, z))
+        near = lax.rem(y + 3 - 2 * side, 4)
+        push(part_b.at[q, rows_of(c, near)], land_b.at[1 - side, q, own(c)],
+             ssem.at[OB], rsem.at[TB, c], (hour, x * 4 + near, z))
+
+    def multiply(c):
         injection(c)
+        where = pl.ds(pl.multiple_of(c * chunk, chunk), block)
 
         @pl.loop(0, 4)
         def _(k):
@@ -138,31 +163,51 @@
             def _():
                 fetch(q, lambda dma: dma.wait())
 
-            flow = product(q, 0)
-            part_a[q, rows(c)] = flow.astype(BF16)
+            flow = product(q * QUARTER, SIDE_A)
+            part_a[q, where] = flow.astype(BF16)
+
+            @pl.when((c == 0) & (k == 0))
+            def _():
+                pl.semaphore_wait(pltpu.get_barrier_semaphore(), 10)
+
+            @pl.when(k == 0)
+            def _():
+                send_far_a(c)
+
+            @pl.when(k == 1)
+            def _():
+                send_near_a(c, 1)
 
             @pl.when(k == 2)
             def _():
-                own_a[rows(c)] = flow
-
-            part_b[q, rows(c)] = product(q, 1).astype(BF16)
-
-        @pl.when(c == 0)
+                own_a[where] = flow
+
+            @pl.when(k == 3)
+            def _():
+                send_near_a(c, 0)
+
+            part_b[q, where] = product(q * QUARTER + SIDE_A, SIDE_B).astype(BF16)
+            send_b(c, q)
+
+    def forward(c):
+        if TOGETHER == 1:
+            multiply(c)
+            return
+
+        @pl.when(lax.rem(c, TOGETHER) == 0)
         def _():
-            pl.semaphore_wait(pltpu.get_barrier_semaphore(), 10)
-
-        for j in range(2):
-            push(part_a.at[at(x, 2), half_rows(c, j)], relay_a.at[half_rows(c, j)],
-                 ssem.at[OA], rsem.at[OA, c], dev_x(j))
-            pair = pl.ds(2 * j, 2)
-            push(part_b.at[pair, rows_of(c, at(y, 2))], relay_b.at[pair, own(c)],
-                 ssem.at[OB], rsem.at[OB, c], dev_y(j))
-        for j in range(2):
-            half = half_rows(c, 1 - j)
-            push(part_a.at[at(x, j), half], land_a.at[j, half], ssem.at[OA], rsem.at[TA, c], dev_x(j))
-            pair = pl.ds(2 - 2 * j, 2)
-            push(part_b.at[pair, rows_of(c, at(y, j))], land_b.at[j, pair, own(c)],
-                 ssem.at[OB], rsem.at[TB, c], dev_y(j))
+            multiply(c)
+
+        @pl.when(lax.rem(c, TOGETHER) != 0)
+        def _():
+            send_far_a(c)
+
+            @pl.loop(0, 4)
+            def _(q):
+                send_b(c, q)
+
+            for j in range(2):
+                send_near_a(c, j)
 
     def relay(c):
         receive(OA, c, relay_a.at[rows(c)])
@@ -239,23 +284,31 @@
         total = total_a(where)
         for j in range(3):
             total = total + land2_a[j, own(c), :].astype(F32)
-        fg[where, 0:HALF] = (scale[:, 0:HALF] * hinge_grad(total, bound[:, 0:HALF])).astype(BF16)
+        fg[where, 0:SIDE_A] = (
+            scale[:, 0:SIDE_A] * hinge_grad(total, bound[:, 0:SIDE_A])
+        ).astype(BF16)
         receive(S2B, c, land2_b.at[:, own(c)])
         total = total_b(c, x)
         for j in range(3):
             total = total + land2_b[j, own(c), :].astype(F32)
-        fg[where, HALF:QUARTER] = (
-            scale[:, HALF:QUARTER] * hinge_grad(total, bound[:, HALF:QUARTER])
+        fg[where, SIDE_A:QUARTER] = (
+            scale[:, SIDE_A:QUARTER] * hinge_grad(total, bound[:, SIDE_A:QUARTER])
         ).astype(BF16)
-        for j in (2, 0, 1):
+        for j in range(2):
             push(fg.at[where], fg.at[where], ssem.at[AGY], rsem.at[AGY, c], dev_y(j))
+
+    def gather_relay(c):
+        receive(AGY, c, fg.at[own_rows(c, 2)])
+        for j in range(2):
+            part = fg.at[rows_of(c, at(y, 1 - j)), pl.ds(j * HALF, HALF)]
+            push(part, part, ssem.at[AGY], rsem.at[AGR, c], dev_y(j))
 
     def step3(c):
         @pl.when(c == 0)
         def _():
             take(g_send, g_sem.at[3])
 
-        receive(AGY, c, fg.at[own_rows(c, 3)])
+        receive(AGR, c, fg.at[own_rows(c, 1)])
 
         @pl.loop(0, 4)
         def _(k):
@@ -393,7 +446,10 @@
     lax.fori_loop(0, hours, generate, 0)
     locals_in[2].wait()
 
-    steps = dict(zip("FR123456", (forward, relay, step1, step2, step3, step4, step5, step6)))
+    steps = dict(
+        F=forward, R=relay, Y=gather_relay,
+        **dict(zip("123456", (step1, step2, step3, step4, step5, step6))),
+    )
 
     def iteration(i, carry):
         for name, lag in ORDER:
@@ -402,11 +458,6 @@
                 def _():
                     locals_in[5].wait()
                     locals_in[6].wait()
-            if name == "3":
-                @pl.when(i == lag)
-                def _():
-                    share_factors()
-
             @pl.when((i >= lag) & (i < CHUNKS + lag))
             def _():
                 steps[name](i - lag)
@@ -415,9 +466,16 @@
                 @pl.when(i == 0)
                 def _():
                     halo().start()
-                    for j in (2, 0, 1):
-                        send_factor(j)
                     own_factor()
+
+        for j in (2, 0, 1):
+            @pl.when(i == FACTORS[j])
+            def _():
+                send_factor(j)
+
+        @pl.when(i == FACTORS[3])
+        def _():
+            share_factors()
 
         return carry
 
@@ -464,18 +522,18 @@
             pltpu.VMEM((hours + 1, scen, units), F32),
             pltpu.VMEM((1, all_lines), F32),
             pltpu.VMEM((1, all_lines), F32),
-            pltpu.VMEM((columns // CHUNKS, nodes), BF16),
-            pltpu.VMEM((4, columns, HALF), BF16),
-            pltpu.VMEM((4, columns, HALF), BF16),
-            pltpu.VMEM((columns, HALF), F32),
-            pltpu.VMEM((columns, HALF), BF16),
-            pltpu.VMEM((4, own, HALF), BF16),
-            pltpu.VMEM((2, columns, HALF), BF16),
-            pltpu.VMEM((2, 4, own, HALF), BF16),
-            pltpu.VMEM((columns, HALF), BF16),
-            pltpu.VMEM((4, own, HALF), BF16),
-            pltpu.VMEM((3, own, HALF), BF16),
-            pltpu.VMEM((3, own, HALF), BF16),
+            pltpu.VMEM((columns // CHUNKS * TOGETHER, nodes), BF16),
+            pltpu.VMEM((4, columns, SIDE_A), BF16),
+            pltpu.VMEM((4, columns, SIDE_B), BF16),
+            pltpu.VMEM((columns, SIDE_A), F32),
+            pltpu.VMEM((columns, SIDE_A), BF16),
+            pltpu.VMEM((4, own, SIDE_B), BF16),
+            pltpu.VMEM((2, columns, SIDE_A), BF16),
+            pltpu.VMEM((2, 4, own, SIDE_B), BF16),
+            pltpu.VMEM((columns, SIDE_A), BF16),
+            pltpu.VMEM((4, own, SIDE_B), BF16),
+            pltpu.VMEM((3, own, SIDE_A), BF16),
+            pltpu.VMEM((3, own, SIDE_B), BF16),
             pltpu.VMEM((columns, QUARTER), BF16),
             pltpu.VMEM((columns, 4 * units), F32),
             pltpu.VMEM((columns, 4 * units), BF16),

time: 112 us -> 106 us (0.946)
  Pallas kernels: 110 us -> 103 us
    pallas_call x1, Pallas kernels: 110 us -> 103 us  [body(): pl.pallas_call(kernel, out_shape=jax.ShapeDtypeStruct((columns, units), F...]
where the time goes in v4:
time: 106 us; the launch traced here: 105 us
  Pallas kernels  103 us (97%)
  local copies, waits for them, and re-layouts  2.06 us (2%)
    pallas_call x1, Pallas kernels, body(): pl.pallas_call(kernel, out_shape=jax.ShapeDtypeStruct((columns, units), F...  103 us

profile of v4, /device:TPU:0, one launch (start us, length us, event | category | flops | bytes accessed | tf_op | source)
XLA Modules:
  0.0 105.4 jit_solution(17160915421169500393)
XLA Ops:
  0.0 103.3 %shard_map.118 = f32[768,256]{1,0:T(8,128)} custom-call(f32[4]{0:T(128)} %levels.1, bf16[4992,1024]{1,0:T(8,128)(2,1)} %ptdf_hbm.1, f32[768,1024]{1,0:T(8,128)} %bitcast.6, f32[96,8,256]{2,1,0:T(8,128)} %units_hbm.1, s32[96,256]{1,0:T(8,128)} %commit_hbm.1, s32[96,4992]{1,0:T(8,128)} %active_hbm.1, s32[192,256]{1,0:T(8,128)} %ramp_hbm.1, f32[4992]{0:T(1024)} %limit_hbm.1, ...), custom_call_target="tpu_custom_call" | custom-call | tf_op jit(solution)/shard_map/pallas_call | solution.py:508
  103.3 2.1 %copy.14 = f32[96,8,256]{2,1,0:T(8,128)} copy(f32[96,8,256]{2,1,0:T(8,128)} %bitcast.5) | data formatting | bytes 1572864

commit v5 on v4

--- a/solution.py
+++ b/solution.py
@@ -12,14 +12,14 @@
 CHUNKS = 6
 TOGETHER = 2
 QUARTER = 1280
-SIDE_A = 512
+SIDE_A = 640
 SIDE_B = QUARTER - SIDE_A
 HALF = QUARTER // 2
 SCEN = 8
-OA, OB, TA, TB, S2A, S2B, AGY, AGR, SUMZ, SUMX, AGZ = range(11)
-KINDS = 11
-ORDER = (("F", 0), ("Y", 6), ("2", 5), ("5", 10), ("4", 8), ("1", 3), ("3", 6), ("R", 1), ("6", 11))
-FACTORS = (1, 3, 2, 5)
+OA, OB, TA, TB, S2A, S2B, AGY, AGR, SUMZ, SUMX, AGZ, SCALE = range(12)
+KINDS = 15
+ORDER = (("F", 0), ("2", 5), ("5", 9), ("1", 3), ("R", 1), ("3", 6), ("6", 12), ("Y", 5), ("4", 7))
+FACTORS = (2, 3, 5)
 
 
 def hinge_grad(values, limits):
@@ -30,8 +30,8 @@
     levels, ptdf_hbm, load_hbm, units_hbm, commit_hbm, active_hbm, ramp_hbm, limit_hbm, weight_hbm,
     node, ramp_limit, ramp_weight, out,
     p, load, units, commit, active, ramp, lev, gx, rw, lim, wgt, inj,
-    part_a, part_b, own_a, relay_a, relay_b, land_a, land_b, sum_a, sum_b, land2_a, land2_b,
-    fg, u, u_send, land_z, sum_z, land_x, ob, onehot, g_send, g,
+    part_a, part_b, own_a, near_a, prod_b, own_b, near_b, relay_a, relay_b, land_a, land_b, sum_a, sum_b, code_a, code_b, land2_a, land2_b,
+    scale, land_scale, fg, u, code_u, land_z, sum_z, land_x, ob, onehot, g_send, g,
     p_sem, in_sem, ssem, rsem, g_sem, halo_sem,
 ):
     columns, nodes = load.shape
@@ -159,23 +159,25 @@
         def _(k):
             q = lax.rem(x + 2 + k, 4)
 
-            @pl.when(c == 0)
+            @pl.when((c == 0) & (k > 0))
             def _():
                 fetch(q, lambda dma: dma.wait())
 
             flow = product(q * QUARTER, SIDE_A)
             part_a[q, where] = flow.astype(BF16)
-
-            @pl.when((c == 0) & (k == 0))
-            def _():
-                pl.semaphore_wait(pltpu.get_barrier_semaphore(), 10)
 
             @pl.when(k == 0)
             def _():
                 send_far_a(c)
 
+            def keep(j):
+                for n in range(TOGETHER):
+                    low = n * chunk + j * (chunk // 2)
+                    near_a[half_rows(c + n, j), :] = flow[low : low + chunk // 2, :]
+
             @pl.when(k == 1)
             def _():
+                keep(1)
                 send_near_a(c, 1)
 
             @pl.when(k == 2)
@@ -184,10 +186,17 @@
 
             @pl.when(k == 3)
             def _():
+                keep(0)
                 send_near_a(c, 0)
 
-            part_b[q, where] = product(q * QUARTER + SIDE_A, SIDE_B).astype(BF16)
+            flow_b = product(q * QUARTER + SIDE_A, SIDE_B)
+            part_b[q, where] = flow_b.astype(BF16)
             send_b(c, q)
+            prod_b[...] = flow_b
+            beside = lax.rem(y + 1 + 2 * (q // 2), 4)
+            for n in range(TOGETHER):
+                own_b[q, own(c + n), :] = prod_b[span(n * chunk + y * sub, sub), :]
+                near_b[q, own(c + n), :] = prod_b[span(n * chunk + beside * sub, sub), :]
 
     def forward(c):
         if TOGETHER == 1:
@@ -209,6 +218,23 @@
             for j in range(2):
                 send_near_a(c, j)
 
+    def encode(n, c, values):
+        most = jnp.maximum(jnp.max(jnp.abs(values), keepdims=True).reshape(1, 1), 1e-30)
+        scale[n, c] = jnp.broadcast_to(most / 32000.0, (8, 128))
+        return 32000.0 / most
+
+    def coded(values, factor):
+        return jnp.round(values * factor).astype(jnp.int32).astype(jnp.int16)
+
+    def decode(n, j, c, codes):
+        return codes.astype(jnp.int32).astype(F32) * land_scale[n, j, c, 0:1, 0:1]
+
+    def send_scale(n, c, j, dev):
+        push(scale.at[n, c], land_scale.at[n, j, c], ssem.at[SCALE + n], rsem.at[SCALE + n, c], dev)
+
+    def receive_scale(n, c):
+        receive(SCALE + n, c, land_scale.at[n, :, c])
+
     def relay(c):
         receive(OA, c, relay_a.at[rows(c)])
         for j in range(2):
@@ -216,7 +242,7 @@
 
             def add_a(where):
                 part_a[q, where, :] = (
-                    part_a[q, where, :].astype(F32) + relay_a[where, :].astype(F32)
+                    near_a[where, :] + relay_a[where, :].astype(F32)
                 ).astype(BF16)
 
             over_rows(c * chunk + j * (chunk // 2), chunk // 2, 16, add_a)
@@ -229,7 +255,7 @@
             @pl.loop(2 * j, 2 * j + 2)
             def _(q):
                 part_b[q, where, :] = (
-                    part_b[q, where, :].astype(F32) + relay_b[q, own(c), :].astype(F32)
+                    near_b[q, own(c), :] + relay_b[q, own(c), :].astype(F32)
                 ).astype(BF16)
 
             pair = pl.ds(2 * j, 2)
@@ -240,29 +266,35 @@
         return own_a[where, :] + land_a[0, where, :].astype(F32) + land_a[1, where, :].astype(F32)
 
     def total_b(c, q):
-        total = part_b[q, rows_of(c, y), :].astype(F32)
+        total = own_b[q, own(c), :]
         for j in range(2):
             total = total + land_b[j, q, own(c), :].astype(F32)
         return total
 
     def step1(c):
         receive(TA, c, land_a.at[:, rows(c)])
-
-        def add_a(where):
-            sum_a[where, :] = total_a(where).astype(BF16)
-
-        over_rows(c * chunk, chunk, 16, add_a)
+        sum_a[...] = total_a(rows(c))
+        factor = encode(0, c, sum_a[...])
+        code_a[rows(c), :] = coded(sum_a[...], factor)
         for j in (2, 0, 1):
-            push(sum_a.at[rows_of(c, at(y, j))], land2_a.at[j, own(c)],
+            send_scale(0, c, j, dev_y(j))
+            push(code_a.at[rows_of(c, at(y, j))], land2_a.at[j, own(c)],
                  ssem.at[S2A], rsem.at[S2A, c], dev_y(j))
         receive(TB, c, land_b.at[:, :, own(c)])
 
         @pl.loop(0, 4)
         def _(q):
-            sum_b[q, own(c), :] = total_b(c, q).astype(BF16)
+            sum_b[span(q * sub, sub), :] = total_b(c, q)
+
+        factor_b = encode(1, c, sum_b[...])
+
+        @pl.loop(0, 4)
+        def _(q):
+            code_b[q, own(c), :] = coded(sum_b[span(q * sub, sub), :], factor_b)
 
         for j in (2, 0, 1):
-            push(sum_b.at[at(x, j), own(c)], land2_b.at[j, own(c)],
+            send_scale(1, c, j, dev_x(j))
+            push(code_b.at[at(x, j), own(c)], land2_b.at[j, own(c)],
                  ssem.at[S2B], rsem.at[S2B, c], dev_x(j))
 
     def step2(c):
@@ -280,17 +312,19 @@
         scale = 2.0 * wgt[:, line] * mask
         bound = lim[:, line]
         where = rows_of(c, y)
+        receive_scale(0, c)
         receive(S2A, c, land2_a.at[:, own(c)])
         total = total_a(where)
         for j in range(3):
-            total = total + land2_a[j, own(c), :].astype(F32)
+            total = total + decode(0, j, c, land2_a[j, own(c), :])
         fg[where, 0:SIDE_A] = (
             scale[:, 0:SIDE_A] * hinge_grad(total, bound[:, 0:SIDE_A])
         ).astype(BF16)
+        receive_scale(1, c)
         receive(S2B, c, land2_b.at[:, own(c)])
         total = total_b(c, x)
         for j in range(3):
-            total = total + land2_b[j, own(c), :].astype(F32)
+            total = total + decode(1, j, c, land2_b[j, own(c), :])
         fg[where, SIDE_A:QUARTER] = (
             scale[:, SIDE_A:QUARTER] * hinge_grad(total, bound[:, SIDE_A:QUARTER])
         ).astype(BF16)
@@ -312,22 +346,28 @@
 
         @pl.loop(0, 4)
         def _(k):
-            grad = jnp.dot(fg[rows(c), :], g[k], preferred_element_type=F32)
-            u[rows(c), unit_lanes(k)] = grad
-            u_send[rows(c), unit_lanes(k)] = grad.astype(BF16)
+            u[rows(c), unit_lanes(k)] = jnp.dot(fg[rows(c), :], g[k], preferred_element_type=F32)
+
+        factor = encode(2, c, u[rows(c), :])
+
+        @pl.loop(0, 4)
+        def _(k):
+            code_u[rows(c), unit_lanes(k)] = coded(u[rows(c), unit_lanes(k)], factor)
 
         for j in (2, 0, 1):
-            push(u_send.at[rows_of(c, at(z, j))], land_z.at[j, own(c)],
+            send_scale(2, c, j, dev_z(j))
+            push(code_u.at[rows_of(c, at(z, j))], land_z.at[j, own(c)],
                  ssem.at[SUMZ], rsem.at[SUMZ, c], dev_z(j))
 
     def step4(c):
+        receive_scale(2, c)
         receive(SUMZ, c, land_z.at[:, own(c)])
 
         @pl.loop(0, 4)
         def _(k):
             total = u[rows_of(c, z), unit_lanes(k)]
             for j in range(3):
-                total = total + land_z[j, own(c), unit_lanes(k)].astype(F32)
+                total = total + decode(2, j, c, land_z[j, own(c), unit_lanes(k)])
             sum_z[own(c), unit_lanes(k)] = total
 
         for j in (2, 0, 1):
@@ -393,28 +433,26 @@
             send_sem=halo_sem.at[0], recv_sem=halo_sem.at[1], device_id=sibling, device_id_type=MESH,
         )
 
+    rest_rows = pl.ds(block, columns - block)
     locals_in = [
         pltpu.make_async_copy(src, dst, in_sem.at[n])
         for n, (src, dst) in enumerate(
             [
                 (commit_hbm, commit),
                 (units_hbm, units),
-                (load_hbm, load),
+                (load_hbm.at[pl.ds(0, block)], load.at[pl.ds(0, block)]),
                 (active_hbm, active.at[:, pl.ds(0, lines)]),
                 (ramp_hbm, ramp),
                 (limit_hbm, lim.at[0, pl.ds(0, lines)]),
                 (weight_hbm, wgt.at[0, pl.ds(0, lines)]),
+                (load_hbm.at[rest_rows], load.at[rest_rows]),
             ]
         )
     ]
     for dma in locals_in[:2]:
         dma.start()
-    for k in range(4):
-        fetch(lax.rem(x + (2, 1, 3, 0)[k], 4), lambda dma: dma.start())
-        if k == 0:
-            locals_in[2].start()
-    for dma in locals_in[3:]:
-        dma.start()
+    fetch(lax.rem(x + 2, 4), lambda dma: dma.start())
+    locals_in[2].start()
     barrier = pltpu.get_barrier_semaphore()
     for j in range(3):
         for dev in (dev_x(j), dev_y(j), dev_z(j)):
@@ -423,15 +461,14 @@
 
     fill = 4 * QUARTER - lines
     p[lines:, :] = jnp.zeros((fill, nodes), BF16)
-    active[:, lines:] = jnp.zeros((hours, fill), jnp.int32)
-    lim[:, lines:] = jnp.zeros((1, fill), F32)
-    wgt[:, lines:] = jnp.zeros((1, fill), F32)
     onehot[...] = (
         lax.broadcasted_iota(jnp.int32, onehot.shape, 0) == node[...] - bus * nodes
     ).astype(F32).astype(BF16)
     gx[(hours + 1) * hour] = jnp.zeros((SCEN, n_units), F32)
     locals_in[0].wait()
     locals_in[1].wait()
+    for k in range(1, 4):
+        fetch(lax.rem(x + 2 + k, 4), lambda dma: dma.start())
 
     def generate(k, carry):
         row = commit[pl.ds(k, 1), :]
@@ -443,7 +480,10 @@
         gx[k + 1] = value * units[k]
         return carry
 
-    lax.fori_loop(0, hours, generate, 0)
+    lax.fori_loop(0, block // SCEN, generate, 0)
+    fetch(lax.rem(x + 2, 4), lambda dma: dma.wait())
+    pl.semaphore_wait(barrier, 10)
+    send_factor(2)
     locals_in[2].wait()
 
     steps = dict(
@@ -465,15 +505,22 @@
             if name == "F":
                 @pl.when(i == 0)
                 def _():
+                    for n in (7, 3, 4, 5, 6):
+                        locals_in[n].start()
+                    lax.fori_loop(block // SCEN, hours, generate, 0)
                     halo().start()
+                    active[:, lines:] = jnp.zeros((hours, fill), jnp.int32)
+                    lim[:, lines:] = jnp.zeros((1, fill), F32)
+                    wgt[:, lines:] = jnp.zeros((1, fill), F32)
                     own_factor()
-
-        for j in (2, 0, 1):
+                    locals_in[7].wait()
+
+        for j in range(2):
             @pl.when(i == FACTORS[j])
             def _():
                 send_factor(j)
 
-        @pl.when(i == FACTORS[3])
+        @pl.when(i == FACTORS[2])
         def _():
             share_factors()
 
@@ -482,6 +529,8 @@
     lax.fori_loop(0, CHUNKS + max(lag for _, lag in ORDER), iteration, 0)
     take(part_a.at[pl.ds(0, 3)], ssem.at[OA])
     take(part_b.at[pl.ds(0, 3)], ssem.at[OB])
+    for n in range(3):
+        take(land_scale.at[n], ssem.at[SCALE + n])
     take(land2_a, ssem.at[S2A])
     take(land2_b, ssem.at[S2B])
     take(fg.at[pl.ds(0, 3 * (columns // 4))], ssem.at[AGY])
@@ -526,18 +575,26 @@
             pltpu.VMEM((4, columns, SIDE_A), BF16),
             pltpu.VMEM((4, columns, SIDE_B), BF16),
             pltpu.VMEM((columns, SIDE_A), F32),
+            pltpu.VMEM((columns, SIDE_A), F32),
+            pltpu.VMEM((columns // CHUNKS * TOGETHER, SIDE_B), F32),
+            pltpu.VMEM((4, own, SIDE_B), F32),
+            pltpu.VMEM((4, own, SIDE_B), F32),
             pltpu.VMEM((columns, SIDE_A), BF16),
             pltpu.VMEM((4, own, SIDE_B), BF16),
             pltpu.VMEM((2, columns, SIDE_A), BF16),
             pltpu.VMEM((2, 4, own, SIDE_B), BF16),
-            pltpu.VMEM((columns, SIDE_A), BF16),
-            pltpu.VMEM((4, own, SIDE_B), BF16),
-            pltpu.VMEM((3, own, SIDE_A), BF16),
-            pltpu.VMEM((3, own, SIDE_B), BF16),
+            pltpu.VMEM((columns // CHUNKS, SIDE_A), F32),
+            pltpu.VMEM((columns // CHUNKS, SIDE_B), F32),
+            pltpu.VMEM((columns, SIDE_A), jnp.int16),
+            pltpu.VMEM((4, own, SIDE_B), jnp.int16),
+            pltpu.VMEM((3, own, SIDE_A), jnp.int16),
+            pltpu.VMEM((3, own, SIDE_B), jnp.int16),
+            pltpu.VMEM((3, CHUNKS, 8, 128), F32),
+            pltpu.VMEM((3, 3, CHUNKS, 8, 128), F32),
             pltpu.VMEM((columns, QUARTER), BF16),
             pltpu.VMEM((columns, 4 * units), F32),
-            pltpu.VMEM((columns, 4 * units), BF16),
-            pltpu.VMEM((3, own, 4 * units), BF16),
+            pltpu.VMEM((columns, 4 * units), jnp.int16),
+            pltpu.VMEM((3, own, 4 * units), jnp.int16),
             pltpu.VMEM((own, 4 * units), F32),
             pltpu.VMEM((3, own, units), F32),
             pltpu.VMEM((columns, units), F32),
@@ -545,14 +602,14 @@
             pltpu.VMEM((3, HALF, units), BF16),
             pltpu.VMEM((4, QUARTER, units), BF16),
             dma((4,)),
-            dma((7,)),
+            dma((8,)),
             dma((KINDS,)),
             dma((KINDS, CHUNKS)),
             dma((4,)),
             dma((2,)),
         ],
         compiler_params=pltpu.CompilerParams(
-            collective_id=0, has_side_effects=True, vmem_limit_bytes=62 << 20
+            collective_id=0, has_side_effects=True, vmem_limit_bytes=63 << 20
         ),
     )(
         relax_levels, ptdf, load.reshape(columns, nodes), units_out, commit_index, line_active,

time: 106 us -> 103 us (0.972)
  Pallas kernels: 103 us -> 101 us
    pallas_call x1, Pallas kernels: 103 us -> 101 us  [body(): pl.pallas_call(kernel, out_shape=jax.ShapeDtypeStruct((columns, units), F...]
where the time goes in v5:
time: 103 us
  Pallas kernels  101 us (98%)
  local copies, waits for them, and re-layouts  2.06 us (2%)
    pallas_call x1, Pallas kernels, body(): pl.pallas_call(kernel, out_shape=jax.ShapeDtypeStruct((columns, units), F...  101 us
    unnamed x1, local copies, waits for them, and re-layouts  2.06 us

profile of v5, /device:TPU:0, one launch (start us, length us, event | category | flops | bytes accessed | tf_op | source)
XLA Modules:
  0.0 102.9 jit_solution(12922272259664535927)
XLA Ops:
  0.0 100.8 %shard_map.118 = f32[768,256]{1,0:T(8,128)} custom-call(f32[4]{0:T(128)} %levels.1, bf16[4992,1024]{1,0:T(8,128)(2,1)} %ptdf_hbm.1, f32[768,1024]{1,0:T(8,128)} %bitcast.6, f32[96,8,256]{2,1,0:T(8,128)} %units_hbm.1, s32[96,256]{1,0:T(8,128)} %commit_hbm.1, s32[96,4992]{1,0:T(8,128)} %active_hbm.1, s32[192,256]{1,0:T(8,128)} %ramp_hbm.1, f32[4992]{0:T(1024)} %limit_hbm.1, ...), custom_call_target="tpu_custom_call" | custom-call | tf_op jit(solution)/shard_map/pallas_call | solution.py:557
  100.8 2.1 %copy.14 = f32[96,8,256]{2,1,0:T(8,128)} copy(f32[96,8,256]{2,1,0:T(8,128)} %bitcast.5) | data formatting | bytes 1572864
